TPU v7x, 256 devices: a whole 4x4x8 slice. The times are simulated.
256 devices in a mesh: dp: 64 (over y, x, z_hi, core), tensor: 4 (over z_lo).
Axes of the slice: x: 4, y: 4, z: 8 (z_hi: 2, z_lo: 4; z = z_hi * 4 + z_lo), core: 2. Of those that a mesh axis runs over, the one named last changes fastest.
Arguments:
- inputs: bfloat16 [32768, 5120], P('dp', 'tensor'), may hold values from -6 to 6
- out_grads: bfloat16 [32768, 27648], P('dp', 'tensor'), may hold values from -6 to 6
- query_inputs: bfloat16 [8192, 5120], P('dp', 'tensor'), may hold values from -6 to 6
- query_grads: bfloat16 [8192, 27648], P('dp', 'tensor'), may hold values from -6 to 6
- in_proj: bfloat16 [5120, 64], P('tensor'), may hold values from -0.078125 to 0.078125
- out_proj: bfloat16 [27648, 64], P('tensor'), may hold values from -0.0390625 to 0.0390625
- doc_ids: int32 [64, 512], P('dp'), may hold values from 0 to 15, never falling along the last dimension, each value on 1 to 64 neighbouring positions
- query_ids: int32 [64, 128], P('dp'), may hold values from 0 to 1, never falling along the last dimension, each value on 1 to 96 neighbouring positions
Outputs:
- scores: float32 [1024, 128], P('dp')
Inputs may be any that keep to these rules, and one draw needn't show every extreme that they name: `doc_ids`: in each row the numbers never fall, and each of the 16 documents has 1 to 64 tokens, one exactly 64. `query_ids`: in each row the numbers never fall, and each of the 2 query documents has 1 to 96 tokens.
All inputs are finite; a program needn't handle non-finite values.
Results may differ from a plain program's by a relative error of at most 0.0046.
Values sent between devices are 32-bit elements; how exact they have to be, the bound alone decides.
A program may use at most 128 MiB of HBM per device.

v0:
```python
import jax
import jax.numpy as jnp
from jax import lax
from jax.sharding import PartitionSpec as P

DOCS_DEV = 16
QDOCS_DEV = 2
ITERS = 3


damping = 0.1


def kron_rows(left, right):
    return (left[:, :, None] * right[:, None, :]).reshape(left.shape[0], -1).astype(jnp.bfloat16)


def doc_sums(row_ids, kron, count):
    onehot = (row_ids[:, None] == jnp.arange(count, dtype=jnp.int32)[None, :]).astype(jnp.bfloat16)
    return jnp.einsum("td,tv->dv", onehot, kron, preferred_element_type=jnp.float32)


def inner_rows(left, right):
    return lax.dot_general(
        left, right, (((0,), (0,)), ((), ())), precision=None, preferred_element_type=jnp.float32
    )


def residual_norm(residual):
    return lax.psum(jnp.sum(residual * residual, axis=0), ("dp", "tensor"))


def local(inputs, out_grads, query_inputs, query_grads, in_proj, out_proj, doc_ids, query_ids):
    highest = lax.Precision.HIGHEST
    ntensor = lax.axis_size("tensor")
    ndp = lax.axis_size("dp")
    tpos = lax.axis_index("tensor")
    dpos = lax.axis_index("dp")
    tok_dev = inputs.shape[0]
    proj = in_proj.shape[1]
    vec = proj * proj
    block = vec // ntensor
    rows = block // ndp
    tokens_all = tok_dev * ndp
    terms = (
        jnp.dot(inputs, in_proj, preferred_element_type=jnp.float32),
        jnp.dot(out_grads, out_proj, preferred_element_type=jnp.float32),
        jnp.dot(query_inputs, in_proj, preferred_element_type=jnp.float32),
        jnp.dot(query_grads, out_proj, preferred_element_type=jnp.float32),
    )
    in_feats, out_feats, query_in, query_out = lax.psum(
        (terms[0], terms[1], terms[2], terms[3]), "tensor"
    )
    kron = kron_rows(in_feats, out_feats)
    kron_block = lax.dynamic_slice_in_dim(kron, tpos * block, block, 1)
    doc_grads = doc_sums(doc_ids[0], kron, DOCS_DEV)
    query_vecs = doc_sums(query_ids[0], kron_rows(query_in, query_out), QDOCS_DEV)
    first_row = tpos * block + dpos * rows
    every = lax.all_gather(query_vecs, "dp", axis=0, tiled=True)
    target = lax.dynamic_slice_in_dim(every, first_row, rows, 1).T
    summed = lax.psum_scatter(inner_rows(kron_block, kron), "dp", scatter_dimension=0, tiled=True)
    columns = lax.broadcasted_iota(jnp.int32, (rows, vec), 1)
    diagonal = lax.broadcasted_iota(jnp.int32, (rows, vec), 0) + first_row
    fisher = summed / tokens_all + damping * (columns == diagonal).astype(jnp.float32)
    solution = jnp.zeros_like(target)
    residual = target
    direction = target
    norms_now = residual_norm(residual)
    for sweep in range(ITERS):
        gathered = lax.all_gather(direction, "dp", axis=0, tiled=True)
        full = lax.all_gather(gathered, "tensor", axis=0, tiled=True)
        image = jnp.dot(fisher, full, precision=highest)
        curvature = lax.psum(jnp.sum(direction * image, axis=0), ("dp", "tensor"))
        step_size = norms_now / curvature
        solution = solution + step_size * direction
        residual = residual - step_size * image
        if sweep + 1 < ITERS:
            norms_next = residual_norm(residual)
            direction = residual + norms_next / norms_now * direction
            norms_now = norms_next
    sol_block = lax.all_gather(solution, "dp", axis=0, tiled=True)
    full_sol = lax.all_gather(sol_block, "tensor", axis=0, tiled=True)
    scores = jnp.dot(doc_grads, full_sol, precision=highest)
    return scores / vec


def solution(mesh):
    return jax.shard_map(
        local,
        mesh=mesh,
        in_specs=(
            P("dp", "tensor"),
            P("dp", "tensor"),
            P("dp", "tensor"),
            P("dp", "tensor"),
            P("tensor", None),
            P("tensor", None),
            P("dp", None),
            P("dp", None),
        ),
        out_specs=P("dp", None),
        check_vma=False,
    )
```

profile of v0, /device:TPU:1, one launch (start us, length us, event | category | flops | bytes accessed | tf_op | source)
XLA Modules:
  0.0 1720.9 jit_solution(17968784199714904270)
XLA Ops:
  6.5 2.0 fusion.36
  8.5 2.5 fusion.37
  11.1 50.2 %all-reduce.6.cloned.1.call-done = (f32[128,64]{0,1:T(8,128)}, f32[128,64]{0,1:T(8,128)}) async-done(((f32[128,64]{0,1:T(8,128)}, f32[128,64]{0,1:T(8,128)}), (f32[128,64]{0,1:T(8,128)}, f32[128,64]{0,1:T(8,128)})) %all-reduce.6.cloned.1.call-update) | async-done | bytes 65552 | tf_op jit(solution)/shard_map/psum | solution.py:51
  61.3 1.1 multiply_convert_fusion.1
  62.4 1.1 convolution_bitcast_fusion
  63.6 2.5 fusion.34
  66.1 5.9 fusion.35
  72.1 77.2 %all-gather.15.cloned.1.call-done = f32[64,2,4096]{2,1,0:T(2,128)} async-done(((f32[1,2,4096]{2,1,0:T(2,128)}), f32[64,2,4096]{2,1,0:T(2,128)}) %all-gather.15.cloned.1.call-update) | async-done | bytes 2097168 | tf_op jit(solution)/shard_map/all_gather | solution.py:59
  149.2 3.7 reshape.22
  152.9 0.9 constant_dynamic-slice_fusion
  153.9 115.3 %all_gather.28 = f32[1024,128]{1,0:T(8,128)} all-gather(f32[16,128]{1,0:T(8,128)S(1)} %bitcast.32), channel_id=1, replica_groups=mesh['dp'=64,'tensor'=4] {'dp'}, dimensions={0}, use_global_device_ids=true | all-gather | bytes 532480 | tf_op jit(solution)/shard_map/all_gather | solution.py:70
  269.2 2.4 multiply_convert_fusion
  271.6 1.9 copy-done.1
  273.6 8.1 fusion.1
  281.8 33.3 %all-gather.7.cloned.1.call-done = f32[4096,128]{1,0:T(8,128)} async-done(((f32[1024,128]{1,0:T(8,128)}), f32[4096,128]{1,0:T(8,128)}) %all-gather.7.cloned.1.call-update) | async-done | bytes 2097168 | tf_op jit(solution)/shard_map/all_gather | solution.py:71
  315.1 509.9 %reduce-scatter.2.cloned.1.call-done = f32[16,4096]{1,0:T(8,128)} async-done(((f32[1024,4096]{1,0:T(8,128)}), f32[16,4096]{1,0:T(8,128)}) %reduce-scatter.2.cloned.1.call-update) | async-done | bytes 262160 | tf_op jit(solution)/shard_map/reduce_scatter | solution.py:61
  825.0 2.9 multiply_reduce_fusion.3
  827.9 89.1 %all-reduce = (f32[128]{0:T(128)S(1)}, f32[128]{0:T(128)S(1)}) all-reduce(f32[128]{0:T(128)S(1)} %get-tuple-element.6, f32[128]{0:T(128)S(1)} %get-tuple-element.5), channel_id=1, replica_groups=mesh['dp'=64,'tensor'=4] {'dp','tensor'}, use_global_device_ids=true, to_apply=%region_5.0 | all-reduce | flops 256 | bytes 2048 | tf_op jit(solution)/shard_map/psum | solution.py:30
  917.0 72.4 %psum.76 = f32[128]{0:T(128)S(1)} all-reduce(f32[128]{0:T(128)S(1)} %get-tuple-element.13), channel_id=1, replica_groups=mesh['dp'=64,'tensor'=4] {'dp','tensor'}, use_global_device_ids=true, to_apply=%region_10.0 | all-reduce | flops 128 | bytes 1024 | tf_op jit(solution)/shard_map/psum | solution.py:30
  989.5 119.8 %all_gather.30 = f32[1024,128]{1,0:T(8,128)} all-gather(f32[16,128]{1,0:T(8,128)S(1)} %multiply_add_fusion.2), channel_id=1, replica_groups=mesh['dp'=64,'tensor'=4] {'dp'}, dimensions={0}, use_global_device_ids=true | all-gather | bytes 532480 | tf_op jit(solution)/shard_map/all_gather | solution.py:70
  1109.4 42.3 %all-gather.9.cloned.1.call-done = f32[4096,128]{1,0:T(8,128)} async-done(((f32[1024,128]{1,0:T(8,128)}), f32[4096,128]{1,0:T(8,128)}) %all-gather.9.cloned.1.call-update) | async-done | bytes 2097168 | tf_op jit(solution)/shard_map/all_gather | solution.py:71
  1151.6 2.8 multiply_reduce_fusion.1
  1154.4 78.7 %psum.77 = f32[128]{0:T(128)S(1)} all-reduce(f32[128]{0:T(128)S(1)} %get-tuple-element.16), channel_id=1, replica_groups=mesh['dp'=64,'tensor'=4] {'dp','tensor'}, use_global_device_ids=true, to_apply=%region_12.0 | all-reduce | flops 128 | bytes 1024 | tf_op jit(solution)/shard_map/psum | solution.py:73
  1233.2 72.3 %psum.78 = f32[128]{0:T(128)S(1)} all-reduce(f32[128]{0:T(128)S(1)} %multiply_reduce_fusion), channel_id=1, replica_groups=mesh['dp'=64,'tensor'=4] {'dp','tensor'}, use_global_device_ids=true, to_apply=%region_14.0 | all-reduce | flops 128 | bytes 1024 | tf_op jit(solution)/shard_map/psum | solution.py:30
  1305.5 118.6 %all_gather.32 = f32[1024,128]{1,0:T(8,128)} all-gather(f32[16,128]{1,0:T(8,128)S(1)} %multiply_add_fusion.1), channel_id=1, replica_groups=mesh['dp'=64,'tensor'=4] {'dp'}, dimensions={0}, use_global_device_ids=true | all-gather | bytes 532480 | tf_op jit(solution)/shard_map/all_gather | solution.py:70
  1424.2 43.4 %all-gather.11.cloned.1.call-done = f32[4096,128]{1,0:T(8,128)} async-done(((f32[1024,128]{1,0:T(8,128)}), f32[4096,128]{1,0:T(8,128)}) %all-gather.11.cloned.1.call-update) | async-done | bytes 2097168 | tf_op jit(solution)/shard_map/all_gather | solution.py:71
  1467.6 2.8 fusion
  1470.4 78.6 %psum.79 = f32[128]{0:T(128)S(1)} all-reduce(f32[128]{0:T(128)S(1)} %fusion), channel_id=1, replica_groups=mesh['dp'=64,'tensor'=4] {'dp','tensor'}, use_global_device_ids=true, to_apply=%region_16.0 | all-reduce | flops 128 | bytes 1024 | tf_op jit(solution)/shard_map/psum | solution.py:73
  1549.0 118.4 %all_gather.34 = f32[1024,128]{1,0:T(8,128)} all-gather(f32[16,128]{1,0:T(8,128)S(1)} %multiply_add_fusion), channel_id=1, replica_groups=mesh['dp'=64,'tensor'=4] {'dp'}, dimensions={0}, use_global_device_ids=true | all-gather | bytes 532480 | tf_op jit(solution)/shard_map/all_gather | solution.py:81
  1667.4 3.5 fusion.6
  1670.9 39.8 %all-gather.13.cloned.1.call-done = f32[4096,128]{1,0:T(8,128)} async-done(((f32[1024,128]{1,0:T(8,128)}), f32[4096,128]{1,0:T(8,128)}) %all-gather.13.cloned.1.call-update) | async-done | bytes 2097168 | tf_op jit(solution)/shard_map/all_gather | solution.py:82
  1710.7 3.3 convolution_multiply_fusion
  (42 shorter events, 0.6 us)
Async XLA Ops:
  6.5 2.0 copy-start
  6.5 55.9 %copy-start.6 = (s32[1,128]{1,0:T(1,128)S(1)}, s32[1,128]{1,0:T(1,128)}, u32[]{:S(2)}) copy-start(s32[1,128]{1,0:T(1,128)} %param.15) | copy-start | bytes 1540
  6.5 54.8 %all-reduce.6.cloned.1.call-start = ((), (), s32[]{:S(2)}) async-start(), calls=%async_computation.7 | async-start | bytes 131072 | tf_op jit(solution)/shard_map/psum | solution.py:51
  8.5 55.0 %copy-start.4 = (bf16[1280,64]{0,1:T(8,128)(2,1)S(1)}, bf16[1280,64]{0,1:T(8,128)(2,1)}, u32[]{:S(2)}) copy-start(bf16[1280,64]{0,1:T(8,128)(2,1)} %param.12) | copy-start | bytes 491524
  11.1 55.0 %copy-start.2 = (bf16[6912,64]{0,1:T(8,128)(2,1)S(1)}, bf16[6912,64]{0,1:T(8,128)(2,1)}, u32[]{:S(2)}) copy-start(bf16[6912,64]{0,1:T(8,128)(2,1)} %param.13) | copy-start | bytes 2654212
  11.1 138.1 %all-gather.15.cloned.1.call-start = ((), (), s32[]{:S(2)}) async-start(), calls=%async_computation.6 | async-start | bytes 2129920 | tf_op jit(solution)/shard_map/all_gather | solution.py:59
  63.5 205.7 %all-reduce.8.cloned.1.call-start = ((), (), s32[]{:S(2)}) async-start(), calls=%async_computation.8 | async-start | bytes 524288 | tf_op jit(solution)/shard_map/psum | solution.py:51
  72.0 243.1 %all-gather.7.cloned.1.call-start = ((), (), s32[]{:S(2)}) async-start(), calls=%async_computation.2 | async-start | bytes 2621440 | tf_op jit(solution)/shard_map/all_gather | solution.py:71
  269.2 555.8 %reduce-scatter.2.cloned.1.call-start = ((), (), s32[]{:S(2)}) async-start(), calls=%async_computation.1 | async-start | bytes 17039360 | tf_op jit(solution)/shard_map/reduce_scatter | solution.py:61
  271.6 1.9 copy-start.1
  281.7 869.9 %all-gather.9.cloned.1.call-start = ((), (), s32[]{:S(2)}) async-start(), calls=%async_computation.3 | async-start | bytes 2621440 | tf_op jit(solution)/shard_map/all_gather | solution.py:71
  825.0 326.7 %copy-start.3 = (f32[16,4096]{1,0:T(8,128)S(1)}, f32[16,4096]{1,0:T(8,128)}, u32[]{:S(2)}) copy-start(f32[16,4096]{1,0:T(8,128)} %reduce-scatter.2.cloned.1.call-done) | copy-start | bytes 786436
  1109.3 358.3 %all-gather.11.cloned.1.call-start = ((), (), s32[]{:S(2)}) async-start(), calls=%async_computation.4 | async-start | bytes 2621440 | tf_op jit(solution)/shard_map/all_gather | solution.py:71
  1424.1 243.3 %copy-start.5 = (s32[1,512]{1,0:T(1,128)S(1)}, s32[1,512]{1,0:T(1,128)}, u32[]{:S(2)}) copy-start(s32[1,512]{1,0:T(1,128)} %param.14) | copy-start | bytes 6148
  1424.1 286.6 %all-gather.13.cloned.1.call-start = ((), (), s32[]{:S(2)}) async-start(), calls=%async_computation.5 | async-start | bytes 2621440 | tf_op jit(solution)/shard_map/all_gather | solution.py:82
Sparse Core Ops, SparseCore 0:
  11.2 50.0 all-reduce.5
  65.4 83.7 all-gather.14
  152.1 41.5 all-reduce.7
  269.3 45.7 all-gather.6
  317.5 507.4 reduce-scatter.1
  1109.4 42.1 all-gather.8
  1424.2 43.3 all-gather.10
  1667.5 43.1 all-gather.12
where the time goes:
time: 1720 us
  blocking collectives  863 us (50%)
  waiting for transfers between devices  796 us (46%)
  matrix products  37.4 us (2%)
    reduce_scatter x1, waiting for transfers between devices, local(): lax.psum_scatter(inner_rows(kron_block, kron), 'dp', scatter_dimension=0,...  510 us
    all_gather x3, blocking collectives, local(): gathered = lax.all_gather(direction, 'dp', axis=0, tiled=True)  354 us
    psum x3, blocking collectives, residual_norm(): return lax.psum(jnp.sum(residual * residual, axis=0), ('dp', 'tensor'))  234 us
    psum x2, blocking collectives, local(): curvature = lax.psum(jnp.sum(direction * image, axis=0), ('dp', 'tensor'))  157 us
    all_gather x3, waiting for transfers between devices, local(): full = lax.all_gather(gathered, 'tensor', axis=0, tiled=True)  119 us
    all_gather x1, blocking collectives, local(): sol_block = lax.all_gather(solution, 'dp', axis=0, tiled=True)  118 us
    all_gather x1, waiting for transfers between devices, local(): every = lax.all_gather(query_vecs, 'dp', axis=0, tiled=True)  77.2 us
    psum x2, waiting for transfers between devices, local(): lax.psum((terms[0], terms[1], terms[2], terms[3]), 'tensor')  50.2 us
  transfers between devices with their start and end apart: 8, of which 7 were waited for; matrix products, arithmetic and copies ran while one was open for 2% of the time, Pallas kernels for 0%

commit v1 on v0

v1 whole, which is shorter than its diff:
```python
import functools

import jax
import jax.numpy as jnp
from jax import lax
from jax.experimental import pallas as pl
from jax.experimental.pallas import tpu as pltpu
from jax.sharding import PartitionSpec as P

MESH = pl.DeviceIdType.MESH
F32, BF16 = jnp.float32, jnp.bfloat16
NT = (((1,), (1,)), ((), ()))
ITERS = 3
DAMPING = 0.1
TILES = 8


def split_bf16(value):
    high = value.astype(BF16)
    return high, (value - high.astype(F32)).astype(BF16)


def query_sum(value):
    return jnp.sum(jnp.sum(value, axis=1), axis=1, keepdims=True)


def kernel(
    tokens_all,
    inp, outg, qinp, qoutg, win, wout, ids, qids,
    out,
    win_v, wout_v, inp_v, outg_v, qinp_v, qoutg_v,
    part, qpart, rs, qrs, ft, rhs1, rhs2, feat_a, lhs, wbuf, acc,
    direction, residual, usend, urecv, rbuf, ssend, srecv, fsend, frecv, order,
    load_sem, rs_send, rs_recv, q_send, q_recv, ring_send, ring_recv, sib_send, sib_recv,
    b_send, b_recv, u_send, u_recv, r_send, r_recv, s_send, s_recv, f_send, f_recv,
):
    dp = lax.axis_index("dp")
    zl = lax.axis_index("tensor")
    core = lax.rem(dp, 2)
    half = lax.rem(dp // 2, 2)
    xy = dp // 4
    xpos = lax.rem(xy, 4)
    ypos = xy // 4
    z = half * 4 + zl
    spot = z * 2 + core

    def plane(index):
        return (index * 4 + half * 2 + core, zl)

    def column(zpos, which):
        return (xy * 4 + (zpos // 4) * 2 + which, lax.rem(zpos, 4))

    def chunk_of(zpos, which):
        return ((zpos // 4) * 2 + which) * 4 + lax.rem(zpos, 4)

    def remote(src, dst, send, recv, device):
        return pltpu.make_async_remote_copy(
            src_ref=src, dst_ref=dst, send_sem=send, recv_sem=recv, device_id=device, device_id_type=MESH
        )

    loads = [
        pltpu.make_async_copy(win, win_v, load_sem.at[0]),
        pltpu.make_async_copy(qinp, qinp_v, load_sem.at[1]),
        pltpu.make_async_copy(wout, wout_v, load_sem.at[2]),
        pltpu.make_async_copy(qoutg, qoutg_v, load_sem.at[3]),
    ]
    for load in loads:
        load.start()

    def chunk_loads(owner):
        rows = pl.ds(pl.multiple_of(owner * 128, 128), 128)
        return (
            pltpu.make_async_copy(inp.at[rows, :], inp_v.at[owner], load_sem.at[4 + owner]),
            pltpu.make_async_copy(outg.at[rows, :], outg_v.at[owner], load_sem.at[8 + owner]),
        )

    for step in range(4):
        for load in chunk_loads(lax.rem(zl + 1 + step, 4)):
            load.start()

    barrier = pltpu.get_barrier_semaphore()

    def greet(step, carry):
        pl.semaphore_signal(barrier, inc=1, device_id=plane(lax.rem(xy + step, 16)), device_id_type=MESH)
        other = lax.rem(spot + step, 16)
        pl.semaphore_signal(
            barrier, inc=1, device_id=column(other // 2, lax.rem(other, 2)), device_id_type=MESH
        )
        return carry

    lax.fori_loop(1, 16, greet, 0)

    for load in loads:
        load.wait()

    def project(left, right):
        return jnp.concatenate(
            [
                jnp.dot(left, win_v[...], preferred_element_type=F32),
                jnp.dot(right, wout_v[...], preferred_element_type=F32),
            ],
            axis=1,
        )

    qpart[...] = project(qinp_v[...], qoutg_v[...])
    pl.semaphore_wait(barrier, 30)
    diag = lax.rem(xpos + ypos, 4)
    query_owner = jnp.where(core == 0, diag, 3 - diag)
    slot = jnp.where(core == 0, zl, 3 - zl)
    owns = zl == query_owner
    q_copy = remote(qpart, qrs.at[zl], q_send, q_recv.at[zl], (dp, query_owner))

    @pl.when(jnp.logical_not(owns))
    def _():
        q_copy.start()

    def rs_copy(owner):
        return remote(part.at[owner], rs.at[zl], rs_send.at[owner], rs_recv.at[zl], (dp, owner))

    def project_chunk(step, carry):
        owner = lax.rem(zl + 1 + step, 4)
        for load in chunk_loads(owner):
            load.wait()
        part[owner] = project(inp_v[owner], outg_v[owner])

        @pl.when(step < 3)
        def _():
            rs_copy(owner).start()

        return carry

    lax.fori_loop(0, 4, project_chunk, 0)

    def b_copy(target):
        rows = pl.ds(pl.multiple_of(ypos * 64, 64), 64)
        return remote(
            direction.at[rows, :], direction.at[rows, :], b_send.at[target], b_recv.at[ypos], plane(target)
        )

    lane = lax.broadcasted_iota(jnp.int32, (128, 128), 1)

    @pl.when(owns)
    def _():
        qrs[zl] = qpart[...]
        for step in range(1, 4):
            source = lax.rem(zl + step, 4)
            remote(qpart, qrs.at[source], q_send, q_recv.at[source], (dp, source)).wait_recv()
        feats = (qrs[0] + qrs[1]) + (qrs[2] + qrs[3])
        turned = feats.T
        right = jnp.concatenate(
            [jnp.where(lane < 64, pltpu.roll(feats, 64, 1), 0.0), jnp.where(lane >= 64, feats, 0.0)], axis=0
        )
        rows = []
        for doc in range(2):
            mask = (qids[...] == doc).astype(F32)
            rows.append(jnp.concatenate([turned[0:32] * mask, turned[32:64] * mask], axis=1))
        left = jnp.concatenate(rows, axis=0)
        direction[pl.ds(pl.multiple_of(ypos * 64, 64), 64), :] = jnp.dot(
            left, right, precision=lax.Precision.HIGHEST, preferred_element_type=F32
        )

        def spread(step, carry):
            b_copy(lax.rem(xy + step, 16)).start()
            return carry

        lax.fori_loop(1, 16, spread, 0)

    rs[zl] = part[zl]
    for step in range(1, 4):
        source = lax.rem(zl + step, 4)
        remote(part.at[source], rs.at[source], rs_send.at[source], rs_recv.at[source], (dp, source)).wait_recv()
    feats = (rs[0] + rs[1]) + (rs[2] + rs[3])
    own = chunk_of(z, core)
    ids_own = jnp.zeros((1, 128), F32)
    for index in range(4):
        ids_own = ids_own + jnp.where(zl == index, ids[:, index * 128 : (index + 1) * 128].astype(F32), 0.0)
    ft[own, 0:128] = feats.T
    ft[own, 128:136] = jnp.broadcast_to(ids_own, (8, 128))

    pieces = (pl.ds(0, 64), pl.ds(64, 72))
    reach = ((4, 3), (3, 4))

    def ring_copy(way, piece, step):
        sign = 1 if way == 0 else 7
        origin = lax.rem(z + 8 * 8 - (sign if way == 0 else -1) * (step - 1), 8)
        where = ft.at[chunk_of(origin, core), pieces[piece], :]
        return remote(
            where, where, ring_send.at[way, piece, step], ring_recv.at[way, piece, step],
            column(lax.rem(z + sign, 8), core),
        )

    def ring_arrival(way, piece, step):
        origin = lax.rem(z + 8 - step, 8) if way == 0 else lax.rem(z + step, 8)
        where = ft.at[chunk_of(origin, core), pieces[piece], :]
        return remote(
            where, where, ring_send.at[way, piece, step], ring_recv.at[way, piece, step],
            column(lax.rem(z + 1, 8), core),
        )

    def sibling_copy(offset, piece, which):
        origin = lax.rem(z + offset, 8)
        where = ft.at[chunk_of(origin, which), pieces[piece], :]
        return remote(
            where, where, sib_send.at[offset, piece], sib_recv.at[offset, piece], column(z, 1 - core)
        )

    for step in range(1, 5):
        for way in range(2):
            for piece in range(2):
                if step > 1 and step - 1 <= reach[way][piece]:
                    ring_arrival(way, piece, step - 1).wait_recv()
                if step <= reach[way][piece]:
                    ring_copy(way, piece, step).start()
        for piece in range(2):
            if step == 1:
                sibling_copy(0, piece, core).start()
            else:
                for way in range(2):
                    if step - 1 <= reach[way][piece]:
                        offset = (8 - (step - 1)) if way == 0 else (step - 1)
                        sibling_copy(offset, piece, core).start()
    for way in range(2):
        for piece in range(2):
            if reach[way][piece] == 4:
                ring_arrival(way, piece, 4).wait_recv()
                sibling_copy(4, piece, core).start()
    for offset in range(8):
        for piece in range(2):
            sibling_copy(offset, piece, 1 - core).wait_recv()

    for source in range(4):
        @pl.when(jnp.logical_not(jnp.logical_and(owns, ypos == source)))
        def _():
            rows = pl.ds(source * 64, 64)
            remote(
                direction.at[rows, :], direction.at[rows, :], b_send.at[0], b_recv.at[source], plane(xy)
            ).wait_recv()

    def prepare(tile, carry):
        both = jnp.concatenate([ft[2 * tile], ft[2 * tile + 1]], axis=1)
        feat_a[tile] = both[0:64]
        high, low = split_bf16(both[64:128])
        zero = jnp.zeros_like(high)
        rhs1[tile] = jnp.concatenate([high, high, low, low], axis=0)
        rhs2[tile] = jnp.concatenate(
            [
                jnp.concatenate([high, zero, low, zero], axis=0),
                jnp.concatenate([zero, high, zero, low], axis=0),
            ],
            axis=1,
        )
        return carry

    lax.fori_loop(0, TILES, prepare, 0)

    lane_row = lax.broadcasted_iota(jnp.int32, (256, 128), 1)
    own_rows = pl.ds(pl.multiple_of(xy * 16, 16), 16)
    query_row = lax.broadcasted_iota(jnp.int32, (8, 1), 0)
    residual[...] = direction[...]
    norms = None
    steps = []
    for sweep in range(ITERS):
        last = sweep == ITERS - 1
        vector = direction[...]
        high = vector.astype(BF16).astype(F32)
        low = vector - high
        first = jnp.where(lane_row < 64, high, pltpu.roll(low, 64, 1)).astype(BF16)
        second = jnp.where(lane_row < 64, pltpu.roll(high, 64, 1), low).astype(BF16)
        lhs[0:256, 0:128] = first
        lhs[0:256, 128:256] = first
        lhs[256:512, 0:128] = second
        lhs[256:512, 128:256] = second
        if not last:
            acc[...] = jnp.zeros_like(acc)

        def product(tile, squares):
            made = jnp.dot(lhs[...], rhs1[tile], preferred_element_type=F32)
            left = feat_a[tile].reshape(2, 1, 32, 256)
            inner = jnp.sum(jnp.sum(made.reshape(2, 8, 32, 256) * left, axis=0), axis=1)
            wbuf[tile, sweep * 8 : sweep * 8 + 8] = inner
            if not last:
                spread = (inner.reshape(1, 8, 1, 256) * left).reshape(2, 256, 256)
                for group in (0, 1):
                    hi, lo = split_bf16(spread[group])
                    right = rhs2[tile, :, group * 256 : (group + 1) * 256]
                    acc[...] += lax.dot_general(hi, right, NT, preferred_element_type=F32)
                    acc[...] += lax.dot_general(lo, right, NT, preferred_element_type=F32)
            square = inner * inner
            return squares + square[:, 0:128] + square[:, 128:256]

        squares = lax.fori_loop(0, TILES, product, jnp.zeros((8, 128), F32))
        cube = vector.reshape(8, 32, 128)
        power = query_sum(cube * cube)
        if sweep == 0:
            norms = power
        if not last:
            image = acc[:, 0:128] + acc[:, 128:256]
            usend[:, 0:16] = image.reshape(16, 16, 128)
            usend[:, 16:24] = jnp.broadcast_to(squares[None], (16, 8, 128))
            urecv[sweep, xy] = usend[xy]

            def u_copy(target, source):
                return remote(
                    usend.at[target], urecv.at[sweep, source], u_send.at[sweep, target],
                    u_recv.at[sweep, source], plane(target),
                )

            def u_start(step, carry):
                u_copy(lax.rem(xy + step, 16), xy).start()
                return carry

            def u_wait(step, carry):
                other = lax.rem(xy + step, 16)
                u_copy(other, other).wait_recv()
                return carry

            def u_done(step, carry):
                u_copy(lax.rem(xy + step, 16), xy).wait_send()
                return carry

            lax.fori_loop(1, 16, u_start, 0)
            lax.fori_loop(1, 16, u_wait, 0)
            total = jnp.sum(urecv[sweep], axis=0)
            squared = jnp.sum(total[16:24], axis=1, keepdims=True)
            step_size = norms / (squared / tokens_all + DAMPING * power)
            steps.append(step_size)
            mine = jnp.sum(jnp.where(query_row == xy // 2, step_size, 0.0), axis=0, keepdims=True)
            own_image = total[0:16] / tokens_all + DAMPING * direction[own_rows, :]
            rbuf[sweep, own_rows, :] = residual[own_rows, :] - mine * own_image

            def r_copy(target, source):
                rows = pl.ds(pl.multiple_of(source * 16, 16), 16)
                return remote(
                    rbuf.at[sweep, rows, :], rbuf.at[sweep, rows, :], r_send.at[sweep, target],
                    r_recv.at[sweep, source], plane(target),
                )

            def r_start(step, carry):
                r_copy(lax.rem(xy + step, 16), xy).start()
                return carry

            def r_wait(step, carry):
                other = lax.rem(xy + step, 16)
                r_copy(other, other).wait_recv()
                return carry

            lax.fori_loop(1, 16, r_start, 0)
            lax.fori_loop(1, 16, r_wait, 0)
            lax.fori_loop(1, 16, u_done, 0)
            left_over = rbuf[sweep]
            residual[...] = left_over
            cube_r = left_over.reshape(8, 32, 128)
            norms_next = query_sum(cube_r * cube_r)
            ratio = norms_next / norms
            direction_next = cube_r + ratio.reshape(8, 1, 1) * cube
            if sweep == 0:
                @pl.when(owns)
                def _():
                    def b_done(step, carry):
                        b_copy(lax.rem(xy + step, 16)).wait_send()
                        return carry

                    lax.fori_loop(1, 16, b_done, 0)

            direction[...] = direction_next.reshape(256, 128)
            norms = norms_next

    ssend[...] = squares
    srecv[xy] = squares

    def s_copy(target, source):
        return remote(ssend, srecv.at[source], s_send.at[target], s_recv.at[source], plane(target))

    def s_start(step, carry):
        s_copy(lax.rem(xy + step, 16), xy).start()
        return carry

    def s_wait(step, carry):
        other = lax.rem(xy + step, 16)
        s_copy(other, other).wait_recv()
        return carry

    lax.fori_loop(1, 16, s_start, 0)

    doc_row = lax.broadcasted_iota(jnp.int32, (128, 128), 0).astype(F32)
    sums = []
    for group in range(4):
        onehot = jnp.concatenate(
            [(doc_row == ft[group * 4 + index, 128:129]).astype(BF16) for index in range(4)], axis=1
        )
        hi, lo = split_bf16(jnp.concatenate([wbuf[2 * group], wbuf[2 * group + 1]], axis=1))
        sums.append(
            lax.dot_general(hi, onehot, NT, preferred_element_type=F32)
            + lax.dot_general(lo, onehot, NT, preferred_element_type=F32)
        )

    lax.fori_loop(1, 16, s_wait, 0)
    squared = jnp.sum(jnp.sum(srecv[...], axis=0), axis=1, keepdims=True)
    steps.append(norms / (squared / tokens_all + DAMPING * power))

    for group in range(4):
        scores = steps[0] * sums[group][0:8] + steps[1] * sums[group][8:16] + steps[2] * sums[group][16:24]
        fsend[group] = scores * (1.0 / 4096)

    def f_slot(zpos, which):
        other = lax.rem(zpos, 4)
        return (jnp.where(which == 0, other, 3 - other) * 2 + zpos // 4) * 2 + which

    frecv[f_slot(z, core)] = fsend[half * 2 + core]

    def f_copy(step, back):
        other = lax.rem(spot + step, 16)
        zpos, which = other // 2, lax.rem(other, 2)
        landing = f_slot(zpos, which) if back else f_slot(z, core)
        return remote(
            fsend.at[(zpos // 4) * 2 + which], frecv.at[landing], f_send.at[step], f_recv.at[landing],
            column(zpos, which),
        )

    def f_start(step, carry):
        f_copy(step, False).start()
        return carry

    def f_wait(step, carry):
        f_copy(step, True).wait_recv()
        return carry

    lax.fori_loop(1, 16, f_start, 0)
    lax.fori_loop(1, 16, f_wait, 0)
    for where in range(16):
        diagonal, rest = where // 4, where % 4
        for row in range(4):
            begin = row * 32 + ((diagonal - row) % 4) * 8 + rest * 2
            order[begin : begin + 2] = frecv[where, 2 * row : 2 * row + 2]
    out[...] = order[...].T[0:16]

    @pl.when(jnp.logical_not(owns))
    def _():
        q_copy.wait_send()

    for step in range(3):
        rs_copy(lax.rem(zl + 1 + step, 4)).wait_send()
    for way in range(2):
        for piece in range(2):
            for step in range(1, reach[way][piece] + 1):
                ring_copy(way, piece, step).wait_send()
    for offset in range(8):
        for piece in range(2):
            sibling_copy(offset, piece, core).wait_send()

    def finish(step, carry):
        other = lax.rem(xy + step, 16)
        for sweep in range(ITERS - 1):
            rows = pl.ds(pl.multiple_of(xy * 16, 16), 16)
            remote(
                rbuf.at[sweep, rows, :], rbuf.at[sweep, rows, :], r_send.at[sweep, other],
                r_recv.at[sweep, xy], plane(other),
            ).wait_send()
        s_copy(other, xy).wait_send()
        f_copy(step, False).wait_send()
        return carry

    lax.fori_loop(1, 16, finish, 0)


def local(inputs, out_grads, query_inputs, query_grads, in_proj, out_proj, doc_ids, query_ids):
    tokens_all = inputs.shape[0] * lax.axis_size("dp")
    hbm = pl.BlockSpec(memory_space=pl.ANY)
    vmem = pl.BlockSpec(memory_space=pltpu.VMEM)
    dma = pltpu.SemaphoreType.DMA
    return pl.pallas_call(
        functools.partial(kernel, float(tokens_all)),
        out_shape=jax.ShapeDtypeStruct((16, 128), F32),
        in_specs=[hbm] * 6 + [vmem] * 2,
        out_specs=vmem,
        scratch_shapes=[
            pltpu.VMEM((1280, 64), BF16),
            pltpu.VMEM((6912, 64), BF16),
            pltpu.VMEM((4, 128, 1280), BF16),
            pltpu.VMEM((4, 128, 6912), BF16),
            pltpu.VMEM((128, 1280), BF16),
            pltpu.VMEM((128, 6912), BF16),
            pltpu.VMEM((4, 128, 128), F32),
            pltpu.VMEM((128, 128), F32),
            pltpu.VMEM((4, 128, 128), F32),
            pltpu.VMEM((4, 128, 128), F32),
            pltpu.VMEM((16, 136, 128), F32),
            pltpu.VMEM((TILES, 256, 256), BF16),
            pltpu.VMEM((TILES, 256, 512), BF16),
            pltpu.VMEM((TILES, 64, 256), F32),
            pltpu.VMEM((512, 256), BF16),
            pltpu.VMEM((TILES, 24, 256), F32),
            pltpu.VMEM((256, 256), F32),
            pltpu.VMEM((256, 128), F32),
            pltpu.VMEM((256, 128), F32),
            pltpu.VMEM((16, 24, 128), F32),
            pltpu.VMEM((2, 16, 24, 128), F32),
            pltpu.VMEM((2, 256, 128), F32),
            pltpu.VMEM((8, 128), F32),
            pltpu.VMEM((16, 8, 128), F32),
            pltpu.VMEM((4, 8, 128), F32),
            pltpu.VMEM((16, 8, 128), F32),
            pltpu.VMEM((128, 128), F32),
            dma((12,)),
            dma((4,)),
            dma((4,)),
            dma,
            dma((4,)),
            dma((2, 2, 5)),
            dma((2, 2, 5)),
            dma((8, 2)),
            dma((8, 2)),
            dma((16,)),
            dma((4,)),
            dma((2, 16)),
            dma((2, 16)),
            dma((2, 16)),
            dma((2, 16)),
            dma((16,)),
            dma((16,)),
            dma((16,)),
            dma((16,)),
        ],
        compiler_params=pltpu.CompilerParams(
            collective_id=0, has_side_effects=True, vmem_limit_bytes=48 * 1024 * 1024
        ),
    )(inputs, out_grads, query_inputs, query_grads, in_proj, out_proj, doc_ids, query_ids)


def solution(mesh):
    return jax.shard_map(
        local,
        mesh=mesh,
        in_specs=(
            P("dp", "tensor"),
            P("dp", "tensor"),
            P("dp", "tensor"),
            P("dp", "tensor"),
            P("tensor", None),
            P("tensor", None),
            P("dp", None),
            P("dp", None),
        ),
        out_specs=P("dp", None),
        check_vma=False,
    )
```

time: 1720 us -> 90.6 us (0.05)
  blocking collectives: 863 us -> 0 us
  waiting for transfers between devices: 796 us -> 0 us
  Pallas kernels: 0 us -> 82.7 us
  matrix products: 37.4 us -> 0 us
    reduce_scatter x1 -> x0, waiting for transfers between devices: 510 us -> none  [local(): lax.psum_scatter(inner_rows(kron_block, kron), 'dp', scatter_dimension=0,...]
    all_gather x4 -> x0, blocking collectives: 472 us -> none  [the longest x3 354 us: local(): gathered = lax.all_gather(direction, 'dp', axis=0, tiled=True)]
    psum x5 -> x0, blocking collectives: 391 us -> none  [the longest x3 234 us: residual_norm(): return lax.psum(jnp.sum(residual * residual, axis=0), ('dp', 'tensor'))]
    all_gather x5 -> x0, waiting for transfers between devices: 236 us -> none  [the longest x3 119 us: local(): full = lax.all_gather(gathered, 'tensor', axis=0, tiled=True)]
    pallas_call x0 -> x1, Pallas kernels: none -> 82.7 us  [local(): pl.pallas_call(functools.partial(kernel, float(tokens_all)), out_shape=ja...]
    psum x2 -> x0, waiting for transfers between devices: 50.2 us -> none  [local(): lax.psum((terms[0], terms[1], terms[2], terms[3]), 'tensor')]
    dot_general x11 -> x0, matrix products: 37.4 us -> none  [the longest x3 8.47 us: local(): image = jnp.dot(fisher, full, precision=highest)]
  transfers between devices with their start and end apart: 8 -> 0, of which waited for: 7 -> 0; matrix products, arithmetic and copies ran while one was open for 2% -> 0% of each run, Pallas kernels for 0% -> 0%
where the time goes in v1:
time: 90.6 us; the launch traced here: 90.4 us
  Pallas kernels  82.7 us (91%)
  local copies, waits for them, and re-layouts  7.7 us (8%)
    pallas_call x1, Pallas kernels, local(): pl.pallas_call(functools.partial(kernel, float(tokens_all)), out_shape=ja...  82.7 us
    unnamed x15, local copies, waits for them, and re-layouts  7.7 us

profile of v1, /device:TPU:1, one launch (start us, length us, event | category | flops | bytes accessed | tf_op | source)
XLA Modules:
  0.0 90.4 jit_solution(4435755562709140184)
XLA Ops:
  0.0 0.0 copy-start.5
  0.0 0.0 copy-start.4
  0.0 0.0 copy-start
  0.0 1.9 %copy.9.win = bf16[1280,64]{1,0:T(8,128)(2,1)} copy(bf16[1280,64]{0,1:T(8,128)(2,1)} %param.12) | data formatting | bytes 327680 | tf_op args[4]
  2.0 1.9 %copy.10.wout = bf16[6912,64]{1,0:T(8,128)(2,1)S(1)} copy(bf16[6912,64]{0,1:T(8,128)(2,1)} %param.13) | data formatting | bytes 1769472 | tf_op args[5]
  3.8 0.0 copy-done.5
  3.9 0.0 copy-done.4
  3.9 0.0 copy-done
  3.9 0.0 copy-start.1
  3.9 1.0 %copy-done.1 = bf16[1280,64]{1,0:T(8,128)(2,1)S(1)} copy-done((bf16[1280,64]{1,0:T(8,128)(2,1)S(1)}, bf16[1280,64]{1,0:T(8,128)(2,1)}, u32[]{:S(2)}) %copy-start.1) | copy-done | bytes 163864
  4.9 0.0 copy-start.2
  4.9 1.3 %copy-done.2 = bf16[512,1280]{1,0:T(8,128)(2,1)S(1)} copy-done((bf16[512,1280]{1,0:T(8,128)(2,1)S(1)}, bf16[512,1280]{1,0:T(8,128)(2,1)}, u32[]{:S(2)}) %copy-start.2) | copy-done | bytes 1310744
  6.2 0.0 copy-start.3
  6.2 1.0 %copy-done.3 = bf16[128,1280]{1,0:T(8,128)(2,1)S(1)} copy-done((bf16[128,1280]{1,0:T(8,128)(2,1)S(1)}, bf16[128,1280]{1,0:T(8,128)(2,1)}, u32[]{:S(2)}) %copy-start.3) | copy-done | bytes 327704
  7.1 82.7 %shard_map.82 = f32[16,128]{1,0:T(8,128)S(1)} custom-call(bf16[512,1280]{1,0:T(8,128)(2,1)S(1)} %copy-done.2, bf16[512,6912]{1,0:T(8,128)(2,1)} %outg.1, bf16[128,1280]{1,0:T(8,128)(2,1)S(1)} %copy-done.3, bf16[128,6912]{1,0:T(8,128)(2,1)S(1)} %copy-done, bf16[1280,64]{1,0:T(8,128)(2,1)S(1)} %copy-done.1, bf16[6912,64]{1,0:T(8,128)(2,1)S(1)} %copy.10.wout, ...), custom_call_target="tpu_custom_call" | custom-call | tf_op jit(solution)/shard_map/pallas_call | solution.py:471
  89.8 0.6 copy.12
Async XLA Ops:
  0.0 3.9 %copy-start.5 = (s32[1,128]{1,0:T(1,128)S(1)}, s32[1,128]{1,0:T(1,128)}, u32[]{:S(2)}) copy-start(s32[1,128]{1,0:T(1,128)} %qids.1) | copy-start | bytes 1540
  0.0 3.9 %copy-start.4 = (s32[1,512]{1,0:T(1,128)S(1)}, s32[1,512]{1,0:T(1,128)}, u32[]{:S(2)}) copy-start(s32[1,512]{1,0:T(1,128)} %ids.1) | copy-start | bytes 6148
  0.0 3.9 %copy-start = (bf16[128,6912]{1,0:T(8,128)(2,1)S(1)}, bf16[128,6912]{1,0:T(8,128)(2,1)}, u32[]{:S(2)}) copy-start(bf16[128,6912]{1,0:T(8,128)(2,1)} %qoutg.1) | copy-start | bytes 5308420
  3.9 1.0 %copy-start.1 = (bf16[1280,64]{1,0:T(8,128)(2,1)S(1)}, bf16[1280,64]{1,0:T(8,128)(2,1)}, u32[]{:S(2)}) copy-start(bf16[1280,64]{1,0:T(8,128)(2,1)} %copy.9.win) | copy-start | bytes 491524
  4.9 1.3 %copy-start.2 = (bf16[512,1280]{1,0:T(8,128)(2,1)S(1)}, bf16[512,1280]{1,0:T(8,128)(2,1)}, u32[]{:S(2)}) copy-start(bf16[512,1280]{1,0:T(8,128)(2,1)} %inp.1) | copy-start | bytes 3932164
  6.2 1.0 %copy-start.3 = (bf16[128,1280]{1,0:T(8,128)(2,1)S(1)}, bf16[128,1280]{1,0:T(8,128)(2,1)}, u32[]{:S(2)}) copy-start(bf16[128,1280]{1,0:T(8,128)(2,1)} %qinp.1) | copy-start | bytes 983044

commit v2 on v0

v2 whole, which is shorter than its diff:
```python
import functools

import jax
import jax.numpy as jnp
from jax import lax
from jax.experimental import pallas as pl
from jax.experimental.pallas import tpu as pltpu
from jax.sharding import PartitionSpec as P

MESH = pl.DeviceIdType.MESH
F32, BF16 = jnp.float32, jnp.bfloat16
NT = (((1,), (1,)), ((), ()))
ITERS = 3
DAMPING = 0.1
TILES = 8


def split_bf16(value):
    high = value.astype(BF16)
    return high, (value - high.astype(F32)).astype(BF16)


def query_sum(value):
    return jnp.sum(jnp.sum(value, axis=1), axis=1, keepdims=True)


def kernel(
    tokens_all,
    inp, outg, qinp, qoutg, win, wout, ids_in, qids_in,
    out,
    ids, qids, win_v, wout_v, inp_v, outg_v, qinp_v, qoutg_v,
    part, qpart, rs, qrs, ft, rhs1, rhs2, feat_a, lhs, wbuf, acc, onehot,
    direction, residual, usend, urecv, rbuf, ssend, srecv, fsend, frecv, order,
    load_sem, rs_send, rs_recv, q_send, q_recv, ag_send, ag_recv, sib_send, sib_recv,
    b_send, b_recv, u_send, u_recv, r_send, r_recv, s_send, s_recv, f_send, f_recv,
):
    dp = lax.axis_index("dp")
    zl = lax.axis_index("tensor")
    low = lax.rem(dp, 4)
    core = lax.rem(dp, 2)
    half = low // 2
    xy = dp // 4
    xpos = lax.rem(xy, 4)
    ypos = xy // 4
    z = half * 4 + zl
    pending = []

    plane = [(lax.rem(xy + step, 16), (lax.rem(dp + 4 * step, 64), zl)) for step in range(1, 16)]
    lows = [low] + [lax.rem(low + step, 4) for step in range(1, 4)]
    zls = [zl] + [lax.rem(zl + step, 4) for step in range(1, 4)]
    column = [(lows[a], zls[b], (dp - low + lows[a], zls[b])) for a in range(4) for b in range(4) if a or b]

    barrier = pltpu.get_barrier_semaphore()
    for index in range(15):
        for device in (plane[index][1], column[index][2]):
            pl.semaphore_signal(barrier, inc=1, device_id=device, device_id_type=MESH)

    def up_column(offset, which=None):
        zpos = lax.rem(z + offset, 8)
        return (xy * 4 + (zpos // 4) * 2 + (core if which is None else which), lax.rem(zpos, 4))

    def remote(src, dst, send, recv, device):
        return pltpu.make_async_remote_copy(
            src_ref=src, dst_ref=dst, send_sem=send, recv_sem=recv, device_id=device, device_id_type=MESH
        )

    loads = [
        pltpu.make_async_copy(win, win_v, load_sem.at[0]),
        pltpu.make_async_copy(qinp, qinp_v, load_sem.at[1]),
        pltpu.make_async_copy(wout, wout_v, load_sem.at[2]),
        pltpu.make_async_copy(qoutg, qoutg_v, load_sem.at[3]),
        pltpu.make_async_copy(ids_in, ids, load_sem.at[12]),
        pltpu.make_async_copy(qids_in, qids, load_sem.at[13]),
    ]
    owners = [zls[2], zls[1], zls[3], zl]
    chunk_loads = []
    for step in range(4):
        rows = pl.ds(pl.multiple_of(owners[step] * 128, 128), 128)
        chunk_loads.append(
            (
                pltpu.make_async_copy(inp.at[rows, :], inp_v.at[step], load_sem.at[4 + step]),
                pltpu.make_async_copy(outg.at[rows, :], outg_v.at[step], load_sem.at[8 + step]),
            )
        )
    for load in loads:
        load.start()
    for step in range(2):
        for load in chunk_loads[step]:
            load.start()

    def project(left, right):
        return jnp.concatenate(
            [
                lax.dot_general(left, win_v[...], NT, preferred_element_type=F32),
                lax.dot_general(right, wout_v[...], NT, preferred_element_type=F32),
            ],
            axis=1,
        )

    def project_chunk(step):
        for load in chunk_loads[step]:
            load.wait()
        part[step] = project(inp_v[step], outg_v[step])

    rs_copies = [
        remote(part.at[step], rs.at[zl], rs_send.at[step], rs_recv.at[zl], (dp, owners[step])) for step in range(3)
    ]
    diag = lax.rem(xpos + ypos, 4)
    query_owner = jnp.where(core == 0, diag, 3 - diag)
    owns = zl == query_owner
    q_copy = remote(qpart, qrs.at[zl], q_send, q_recv.at[zl], (dp, query_owner))

    for load in loads:
        load.wait()
    for step in range(2, 4):
        for load in chunk_loads[step]:
            load.start()
    qpart[...] = project(qinp_v[...], qoutg_v[...])
    project_chunk(0)
    pl.semaphore_wait(barrier, 30)

    @pl.when(jnp.logical_not(owns))
    def _():
        q_copy.start()

    rs_copies[0].start()
    for step in range(1, 3):
        project_chunk(step)
        rs_copies[step].start()
    project_chunk(3)
    rs[zl] = part[3]

    def first_done():
        @pl.when(jnp.logical_not(owns))
        def _():
            q_copy.wait_send()

        for copy in rs_copies:
            copy.wait_send()

    pending.append(first_done)

    lane = lax.broadcasted_iota(jnp.int32, (128, 128), 1)
    pair_rows = pl.ds(pl.multiple_of(ypos * 64, 64), 64)
    b_copies = [
        remote(direction.at[pair_rows, :], direction.at[pair_rows, :], b_send.at[index], b_recv.at[ypos], device)
        for index, (_, device) in enumerate(plane)
    ]

    @pl.when(owns)
    def _():
        qrs[zl] = qpart[...]
        for step in range(1, 4):
            remote(qpart, qrs.at[zls[step]], q_send, q_recv.at[zls[step]], (dp, zls[step])).wait_recv()
        feats = (qrs[0] + qrs[1]) + (qrs[2] + qrs[3])
        turned = feats.T
        right = jnp.concatenate(
            [jnp.where(lane < 64, pltpu.roll(feats, 64, 1), 0.0), jnp.where(lane >= 64, feats, 0.0)], axis=0
        )
        rows = []
        for doc in range(2):
            mask = (qids[...] == doc).astype(F32)
            rows.append(jnp.concatenate([turned[0:32] * mask, turned[32:64] * mask], axis=1))
        direction[pair_rows, :] = jnp.dot(
            jnp.concatenate(rows, axis=0), right, precision=lax.Precision.HIGHEST, preferred_element_type=F32
        )
        for copy in b_copies:
            copy.start()

    ids_own = jnp.zeros((1, 128), F32)
    for index in range(4):
        ids_own = ids_own + jnp.where(zl == index, ids[:, index * 128 : (index + 1) * 128].astype(F32), 0.0)
    own = z * 2 + core
    ft[own, 128:136] = jnp.broadcast_to(ids_own, (8, 128))
    for step in range(1, 4):
        remote(part.at[0], rs.at[zls[step]], rs_send.at[0], rs_recv.at[zls[step]], (dp, zls[step])).wait_recv()
    ft[own, 0:128] = ((rs[0] + rs[1]) + (rs[2] + rs[3])).T

    whole, upper, lower = pl.ds(0, 136), pl.ds(0, 64), pl.ds(64, 72)

    def handed(index, origin, rows, target):
        where = ft.at[lax.rem(z + origin, 8) * 2 + core, rows, :]
        return remote(where, where, ag_send.at[index], ag_recv.at[index], up_column(target))

    def sibling(index, origin, rows, back=False):
        where = ft.at[lax.rem(z + origin, 8) * 2 + (1 - core if back else core), rows, :]
        return remote(where, where, sib_send.at[index], sib_recv.at[index], up_column(0, 1 - core))

    arrivals = ((6, whole), (2, whole), (7, whole), (1, whole), (5, whole), (3, whole), (4, upper), (4, lower))
    sent = []

    def start(copy):
        copy.start()
        sent.append(copy)

    start(handed(0, 0, whole, 2))
    start(handed(1, 0, whole, 6))
    start(handed(2, 0, whole, 1))
    start(handed(3, 0, whole, 7))
    start(sibling(8, 0, whole))

    def arrive(index):
        origin, rows = arrivals[index]
        handed(index, origin, rows, 1).wait_recv()

    def pass_on(index):
        origin, rows = arrivals[index]
        start(sibling(index, origin, rows))

    arrive(0)
    start(handed(4, 6, whole, 1))
    start(handed(6, 6, upper, 2))
    pass_on(0)
    arrive(1)
    start(handed(5, 2, whole, 7))
    start(handed(7, 2, lower, 6))
    pass_on(1)
    for index in (2, 3):
        arrive(index)
        pass_on(index)

    def prepare(tile):
        both = jnp.concatenate([ft[2 * tile], ft[2 * tile + 1]], axis=1)
        feat_a[tile] = both[0:64]
        high, rest = split_bf16(both[64:128])
        zero = jnp.zeros_like(high)
        rhs1[tile] = jnp.concatenate([high, high, rest, rest], axis=0)
        rhs2[tile] = jnp.concatenate(
            [
                jnp.concatenate([high, zero, rest, zero], axis=0),
                jnp.concatenate([zero, high, zero, rest], axis=0),
            ],
            axis=1,
        )

    def sibling_tile(index, origin, rows=whole):
        sibling(index, origin, rows, True).wait_recv()

    near = [(8, 0), (0, 6), (1, 2), (2, 7), (3, 1)]
    for index, origin in near:
        sibling_tile(index, origin)
        prepare(lax.rem(z + origin, 8))

    for source in range(4):
        @pl.when(jnp.logical_not(jnp.logical_and(owns, ypos == source)))
        def _():
            rows = pl.ds(source * 64, 64)
            remote(
                direction.at[rows, :], direction.at[rows, :], b_send.at[0], b_recv.at[source], plane[0][1]
            ).wait_recv()

    lane_row = lax.broadcasted_iota(jnp.int32, (256, 128), 1)
    own_rows = pl.ds(pl.multiple_of(xy * 16, 16), 16)
    query_row = lax.broadcasted_iota(jnp.int32, (8, 1), 0)
    doc_row = lax.broadcasted_iota(jnp.int32, (128, 128), 0).astype(F32)

    def set_lhs(vector):
        high = vector.astype(BF16).astype(F32)
        rest = vector - high
        first = jnp.where(lane_row < 64, high, pltpu.roll(rest, 64, 1)).astype(BF16)
        second = jnp.where(lane_row < 64, pltpu.roll(high, 64, 1), rest).astype(BF16)
        lhs[0:256, 0:128] = first
        lhs[0:256, 128:256] = first
        lhs[256:512, 0:128] = second
        lhs[256:512, 128:256] = second

    def product(tile, squares, fresh, back):
        made = jnp.dot(lhs[...], rhs1[tile], preferred_element_type=F32)
        left = feat_a[tile].reshape(2, 1, 32, 256)
        inner = jnp.sum(jnp.sum(made.reshape(2, 8, 32, 256) * left, axis=0), axis=1)
        wbuf[tile] = inner
        if back:
            spread = (inner.reshape(1, 8, 1, 256) * left).reshape(2, 256, 256).astype(BF16)
            image = lax.dot_general(
                jnp.concatenate([spread[0], spread[1]], axis=1), rhs2[tile], NT, preferred_element_type=F32
            )
            if fresh:
                acc[...] = image
            else:
                acc[...] += image
        square = inner * inner
        return squares + square[:, 0:128] + square[:, 128:256]

    def document_sums():
        sums = []
        for group in range(4):
            side = pl.ds((group % 2) * 128, 128)
            tiles = [wbuf[(group // 2) * 4 + index, :, side] for index in range(4)]
            every = jnp.concatenate(tiles, axis=1)
            high = every.astype(BF16).astype(F32)
            both = jnp.concatenate([high, every - high], axis=0).astype(BF16)
            made = lax.dot_general(both, onehot[group], NT, preferred_element_type=F32)
            sums.append(made[0:8] + made[8:16])
        return sums

    def send_all(copies):
        for copy in copies:
            copy.start()

    def sent_all(copies):
        for copy in copies:
            copy.wait_send()

    residual[...] = direction[...]
    norms = None
    scores = None
    for sweep in range(ITERS):
        last = sweep == ITERS - 1
        vector = direction[...]
        set_lhs(vector)
        squares = jnp.zeros((8, 128), F32)
        if sweep == 0:
            for place, (_, origin) in enumerate(near):
                squares = product(lax.rem(z + origin, 8), squares, place == 0, True)
            for index in range(4, 8):
                arrive(index)
                pass_on(index)
            sibling_tile(4, 5)
            prepare(lax.rem(z + 5, 8))
            sibling_tile(5, 3)
            prepare(lax.rem(z + 3, 8))
            sibling_tile(6, 4, upper)
            sibling_tile(7, 4, lower)
            prepare(lax.rem(z + 4, 8))
            for origin in (5, 3, 4):
                squares = product(lax.rem(z + origin, 8), squares, False, True)
        else:
            for tile in range(TILES):
                squares = product(tile, squares, tile == 0, not last)
        cube = vector.reshape(8, 32, 128)
        if not last:
            image = acc[:, 0:128] + acc[:, 128:256]
            usend[:, 0:16] = image.reshape(16, 16, 128)
            usend[:, 16:24] = jnp.broadcast_to(squares[None], (16, 8, 128))
            u_copies = [
                remote(usend.at[target], urecv.at[sweep, xy], u_send.at[sweep, index], u_recv.at[sweep, xy], device)
                for index, (target, device) in enumerate(plane)
            ]
            send_all(u_copies)
            urecv[sweep, xy] = usend[xy]
            if sweep == 0:
                for group in range(4):
                    for index in range(4):
                        chunk = ((group // 2) * 4 + index) * 2 + group % 2
                        onehot[group, :, index * 128 : (index + 1) * 128] = (doc_row == ft[chunk, 128:129]).astype(BF16)
            sums = document_sums()
            power = query_sum(cube * cube)
            if sweep == 0:
                norms = power
            for source, device in plane:
                remote(
                    usend.at[0], urecv.at[sweep, source], u_send.at[sweep, 0], u_recv.at[sweep, source], device
                ).wait_recv()
            total = jnp.sum(urecv[sweep], axis=0)
            squared = jnp.sum(total[16:24], axis=1, keepdims=True)
            step_size = norms / (squared / tokens_all + DAMPING * power)
            mine = jnp.sum(jnp.where(query_row == xy // 2, step_size, 0.0), axis=0, keepdims=True)
            own_image = total[0:16] / tokens_all + DAMPING * direction[own_rows, :]
            rbuf[sweep, own_rows, :] = residual[own_rows, :] - mine * own_image
            r_copies = [
                remote(
                    rbuf.at[sweep, own_rows, :], rbuf.at[sweep, own_rows, :], r_send.at[sweep, index],
                    r_recv.at[sweep, xy], device,
                )
                for index, (_, device) in enumerate(plane)
            ]
            send_all(r_copies)
            pending.append(functools.partial(sent_all, r_copies))
            terms = [step_size * value for value in sums]
            scores = terms if scores is None else [a + b for a, b in zip(scores, terms)]
            sent_all(u_copies)
            if sweep == 0:
                @pl.when(owns)
                def _():
                    sent_all(b_copies)

            for source, device in plane:
                rows = pl.ds(pl.multiple_of(source * 16, 16), 16)
                remote(
                    rbuf.at[sweep, rows, :], rbuf.at[sweep, rows, :], r_send.at[sweep, 0],
                    r_recv.at[sweep, source], device,
                ).wait_recv()
            left_over = rbuf[sweep]
            residual[...] = left_over
            cube_r = left_over.reshape(8, 32, 128)
            norms_next = query_sum(cube_r * cube_r)
            ratio = norms_next / norms
            direction[...] = (cube_r + ratio.reshape(8, 1, 1) * cube).reshape(256, 128)
            norms = norms_next

    ssend[...] = squares
    s_copies = [
        remote(ssend, srecv.at[xy], s_send.at[index], s_recv.at[xy], device)
        for index, (_, device) in enumerate(plane)
    ]
    send_all(s_copies)
    pending.append(functools.partial(sent_all, s_copies))
    srecv[xy] = squares
    power = query_sum(cube * cube)
    sums = document_sums()
    for source, device in plane:
        remote(ssend, srecv.at[source], s_send.at[0], s_recv.at[source], device).wait_recv()
    squared = jnp.sum(jnp.sum(srecv[...], axis=0), axis=1, keepdims=True)
    step_size = norms / (squared / tokens_all + DAMPING * power)

    for group in range(4):
        fsend[group] = (scores[group] + step_size * sums[group]) * (1.0 / 4096)

    def f_slot(where, height):
        return jnp.where(lax.rem(where, 2) == 0, height, 3 - height) * 4 + where

    own_slot = f_slot(low, zl)
    f_copies = [
        remote(fsend.at[where], frecv.at[own_slot], f_send.at[index], f_recv.at[own_slot], device)
        for index, (where, _, device) in enumerate(column)
    ]
    send_all(f_copies)
    pending.append(functools.partial(sent_all, f_copies))
    frecv[own_slot] = fsend[low]
    for copy in sent:
        copy.wait_send()
    for done in pending:
        done()
    for where, height, device in column:
        slot = f_slot(where, height)
        remote(fsend.at[0], frecv.at[slot], f_send.at[0], f_recv.at[slot], device).wait_recv()
    for where in range(16):
        diagonal, rest = where // 4, where % 4
        for row in range(4):
            begin = row * 32 + ((diagonal - row) % 4) * 8 + rest * 2
            order[begin : begin + 2] = frecv[where, 2 * row : 2 * row + 2]
    out[...] = order[...].T[0:16]


def local(inputs, out_grads, query_inputs, query_grads, in_proj, out_proj, doc_ids, query_ids):
    tokens_all = inputs.shape[0] * lax.axis_size("dp")
    hbm = pl.BlockSpec(memory_space=pltpu.HBM)
    vmem = pl.BlockSpec(memory_space=pltpu.VMEM)
    dma = pltpu.SemaphoreType.DMA
    return pl.pallas_call(
        functools.partial(kernel, float(tokens_all)),
        out_shape=jax.ShapeDtypeStruct((16, 128), F32),
        in_specs=[hbm] * 8,
        out_specs=vmem,
        scratch_shapes=[
            pltpu.VMEM((1, 512), jnp.int32),
            pltpu.VMEM((1, 128), jnp.int32),
            pltpu.VMEM((64, 1280), BF16),
            pltpu.VMEM((64, 6912), BF16),
            pltpu.VMEM((4, 128, 1280), BF16),
            pltpu.VMEM((4, 128, 6912), BF16),
            pltpu.VMEM((128, 1280), BF16),
            pltpu.VMEM((128, 6912), BF16),
            pltpu.VMEM((4, 128, 128), F32),
            pltpu.VMEM((128, 128), F32),
            pltpu.VMEM((4, 128, 128), F32),
            pltpu.VMEM((4, 128, 128), F32),
            pltpu.VMEM((16, 136, 128), F32),
            pltpu.VMEM((TILES, 256, 256), BF16),
            pltpu.VMEM((TILES, 256, 512), BF16),
            pltpu.VMEM((TILES, 64, 256), F32),
            pltpu.VMEM((512, 256), BF16),
            pltpu.VMEM((TILES, 8, 256), F32),
            pltpu.VMEM((256, 256), F32),
            pltpu.VMEM((4, 128, 512), BF16),
            pltpu.VMEM((256, 128), F32),
            pltpu.VMEM((256, 128), F32),
            pltpu.VMEM((16, 24, 128), F32),
            pltpu.VMEM((2, 16, 24, 128), F32),
            pltpu.VMEM((2, 256, 128), F32),
            pltpu.VMEM((8, 128), F32),
            pltpu.VMEM((16, 8, 128), F32),
            pltpu.VMEM((4, 8, 128), F32),
            pltpu.VMEM((16, 8, 128), F32),
            pltpu.VMEM((128, 128), F32),
            dma((14,)),
            dma((4,)),
            dma((4,)),
            dma,
            dma((4,)),
            dma((8,)),
            dma((8,)),
            dma((9,)),
            dma((9,)),
            dma((16,)),
            dma((4,)),
            dma((2, 16)),
            dma((2, 16)),
            dma((2, 16)),
            dma((2, 16)),
            dma((16,)),
            dma((16,)),
            dma((16,)),
            dma((16,)),
        ],
        compiler_params=pltpu.CompilerParams(
            collective_id=0, has_side_effects=True, vmem_limit_bytes=62 * 1024 * 1024
        ),
    )(inputs, out_grads, query_inputs, query_grads, in_proj.T, out_proj.T, doc_ids, query_ids)


def solution(mesh):
    return jax.shard_map(
        local,
        mesh=mesh,
        in_specs=(
            P("dp", "tensor"),
            P("dp", "tensor"),
            P("dp", "tensor"),
            P("dp", "tensor"),
            P("tensor", None),
            P("tensor", None),
            P("dp", None),
            P("dp", None),
        ),
        out_specs=P("dp", None),
        check_vma=False,
    )
```

time: 1720 us -> 70 us (0.04)
  blocking collectives: 863 us -> 0 us
  waiting for transfers between devices: 796 us -> 0 us
  Pallas kernels: 0 us -> 68.6 us
  matrix products: 37.4 us -> 0 us
    reduce_scatter x1 -> x0, waiting for transfers between devices: 510 us -> none  [local(): lax.psum_scatter(inner_rows(kron_block, kron), 'dp', scatter_dimension=0,...]
    all_gather x4 -> x0, blocking collectives: 472 us -> none  [the longest x3 354 us: local(): gathered = lax.all_gather(direction, 'dp', axis=0, tiled=True)]
    psum x5 -> x0, blocking collectives: 391 us -> none  [the longest x3 234 us: residual_norm(): return lax.psum(jnp.sum(residual * residual, axis=0), ('dp', 'tensor'))]
    all_gather x5 -> x0, waiting for transfers between devices: 236 us -> none  [the longest x3 119 us: local(): full = lax.all_gather(gathered, 'tensor', axis=0, tiled=True)]
    pallas_call x0 -> x1, Pallas kernels: none -> 68.6 us  [local(): pl.pallas_call(functools.partial(kernel, float(tokens_all)), out_shape=ja...]
    psum x2 -> x0, waiting for transfers between devices: 50.2 us -> none  [local(): lax.psum((terms[0], terms[1], terms[2], terms[3]), 'tensor')]
    dot_general x11 -> x0, matrix products: 37.4 us -> none  [the longest x3 8.47 us: local(): image = jnp.dot(fisher, full, precision=highest)]
  transfers between devices with their start and end apart: 8 -> 0, of which waited for: 7 -> 0; matrix products, arithmetic and copies ran while one was open for 2% -> 0% of each run, Pallas kernels for 0% -> 0%
where the time goes in v2:
time: 70 us; the launch traced here: 69.9 us
  Pallas kernels  68.6 us (98%)
  local copies, waits for them, and re-layouts  1.3 us (2%)
    pallas_call x1, Pallas kernels, local(): pl.pallas_call(functools.partial(kernel, float(tokens_all)), out_shape=ja...  68.6 us

profile of v2, /device:TPU:1, one launch (start us, length us, event | category | flops | bytes accessed | tf_op | source)
XLA Modules:
  0.0 69.9 jit_solution(2275513581177493600)
XLA Ops:
  0.0 68.6 %shard_map.82 = f32[16,128]{1,0:T(8,128)} custom-call(bf16[512,1280]{1,0:T(8,128)(2,1)} %inp.1, bf16[512,6912]{1,0:T(8,128)(2,1)} %outg.1, bf16[128,1280]{1,0:T(8,128)(2,1)} %qinp.1, bf16[128,6912]{1,0:T(8,128)(2,1)} %qoutg.1, bf16[64,1280]{1,0:T(8,128)(2,1)} %bitcast.3, bf16[64,6912]{1,0:T(8,128)(2,1)} %bitcast.2, s32[1,512]{1,0:T(1,128)} %ids_in.1, ...), custom_call_target="tpu_custom_call" | custom-call | tf_op jit(solution)/shard_map/pallas_call | solution.py:440
  68.6 1.3 %copy.10 = f32[16,128]{1,0:T(8,128)} copy(f32[16,128]{1,0:T(8,128)} %shard_map.82) | data formatting | bytes 16384

commit v3 on v2

--- a/solution.py
+++ b/solution.py
@@ -82,11 +82,13 @@
                 pltpu.make_async_copy(outg.at[rows, :], outg_v.at[step], load_sem.at[8 + step]),
             )
         )
-    for load in loads:
-        load.start()
-    for step in range(2):
-        for load in chunk_loads[step]:
+    loads[0].start()
+    loads[2].start()
+    for pair in chunk_loads:
+        for load in pair:
             load.start()
+    for index in (1, 3, 4, 5):
+        loads[index].start()
 
     def project(left, right):
         return jnp.concatenate(
@@ -110,23 +112,23 @@
     owns = zl == query_owner
     q_copy = remote(qpart, qrs.at[zl], q_send, q_recv.at[zl], (dp, query_owner))
 
-    for load in loads:
-        load.wait()
-    for step in range(2, 4):
-        for load in chunk_loads[step]:
-            load.start()
+    loads[0].wait()
+    loads[2].wait()
+    project_chunk(0)
+    project_chunk(1)
+    pl.semaphore_wait(barrier, 30)
+    rs_copies[0].start()
+    rs_copies[1].start()
+    project_chunk(2)
+    rs_copies[2].start()
+    for index in (1, 3, 4, 5):
+        loads[index].wait()
     qpart[...] = project(qinp_v[...], qoutg_v[...])
-    project_chunk(0)
-    pl.semaphore_wait(barrier, 30)
 
     @pl.when(jnp.logical_not(owns))
     def _():
         q_copy.start()
 
-    rs_copies[0].start()
-    for step in range(1, 3):
-        project_chunk(step)
-        rs_copies[step].start()
     project_chunk(3)
     rs[zl] = part[3]
 
@@ -139,6 +141,38 @@
             copy.wait_send()
 
     pending.append(first_done)
+
+    ids_own = jnp.zeros((1, 128), F32)
+    for index in range(4):
+        ids_own = ids_own + jnp.where(zl == index, ids[:, index * 128 : (index + 1) * 128].astype(F32), 0.0)
+    own = z * 2 + core
+    ft[own, 128:136] = jnp.broadcast_to(ids_own, (8, 128))
+    for step in range(1, 4):
+        remote(part.at[0], rs.at[zls[step]], rs_send.at[0], rs_recv.at[zls[step]], (dp, zls[step])).wait_recv()
+    ft[own, 0:128] = ((rs[0] + rs[1]) + (rs[2] + rs[3])).T
+
+    whole, upper, lower = pl.ds(0, 136), pl.ds(0, 64), pl.ds(64, 72)
+
+    def handed(index, origin, rows, target):
+        where = ft.at[lax.rem(z + origin, 8) * 2 + core, rows, :]
+        return remote(where, where, ag_send.at[index], ag_recv.at[index], up_column(target))
+
+    def sibling(index, origin, rows, back=False):
+        where = ft.at[lax.rem(z + origin, 8) * 2 + (1 - core if back else core), rows, :]
+        return remote(where, where, sib_send.at[index], sib_recv.at[index], up_column(0, 1 - core))
+
+    arrivals = ((6, whole), (2, whole), (7, whole), (1, whole), (5, whole), (3, whole), (4, upper), (4, lower))
+    sent = []
+
+    def start(copy):
+        copy.start()
+        sent.append(copy)
+
+    start(handed(0, 0, whole, 2))
+    start(handed(1, 0, whole, 6))
+    start(handed(2, 0, whole, 1))
+    start(handed(3, 0, whole, 7))
+    start(sibling(8, 0, whole))
 
     lane = lax.broadcasted_iota(jnp.int32, (128, 128), 1)
     pair_rows = pl.ds(pl.multiple_of(ypos * 64, 64), 64)
@@ -167,38 +201,6 @@
         for copy in b_copies:
             copy.start()
 
-    ids_own = jnp.zeros((1, 128), F32)
-    for index in range(4):
-        ids_own = ids_own + jnp.where(zl == index, ids[:, index * 128 : (index + 1) * 128].astype(F32), 0.0)
-    own = z * 2 + core
-    ft[own, 128:136] = jnp.broadcast_to(ids_own, (8, 128))
-    for step in range(1, 4):
-        remote(part.at[0], rs.at[zls[step]], rs_send.at[0], rs_recv.at[zls[step]], (dp, zls[step])).wait_recv()
-    ft[own, 0:128] = ((rs[0] + rs[1]) + (rs[2] + rs[3])).T
-
-    whole, upper, lower = pl.ds(0, 136), pl.ds(0, 64), pl.ds(64, 72)
-
-    def handed(index, origin, rows, target):
-        where = ft.at[lax.rem(z + origin, 8) * 2 + core, rows, :]
-        return remote(where, where, ag_send.at[index], ag_recv.at[index], up_column(target))
-
-    def sibling(index, origin, rows, back=False):
-        where = ft.at[lax.rem(z + origin, 8) * 2 + (1 - core if back else core), rows, :]
-        return remote(where, where, sib_send.at[index], sib_recv.at[index], up_column(0, 1 - core))
-
-    arrivals = ((6, whole), (2, whole), (7, whole), (1, whole), (5, whole), (3, whole), (4, upper), (4, lower))
-    sent = []
-
-    def start(copy):
-        copy.start()
-        sent.append(copy)
-
-    start(handed(0, 0, whole, 2))
-    start(handed(1, 0, whole, 6))
-    start(handed(2, 0, whole, 1))
-    start(handed(3, 0, whole, 7))
-    start(sibling(8, 0, whole))
-
     def arrive(index):
         origin, rows = arrivals[index]
         handed(index, origin, rows, 1).wait_recv()
@@ -292,6 +294,11 @@
             made = lax.dot_general(both, onehot[group], NT, preferred_element_type=F32)
             sums.append(made[0:8] + made[8:16])
         return sums
+
+    def own_query(values):
+        return jnp.sum(jnp.where(query_row == xy // 2, values, 0.0), axis=0, keepdims=True)
+
+    message = pl.ds(0, 17)
 
     def send_all(copies):
         for copy in copies:
@@ -331,13 +338,14 @@
         if not last:
             image = acc[:, 0:128] + acc[:, 128:256]
             usend[:, 0:16] = image.reshape(16, 16, 128)
-            usend[:, 16:24] = jnp.broadcast_to(squares[None], (16, 8, 128))
+            for index in range(16):
+                usend[index, 16:17] = squares[index // 2 : index // 2 + 1]
             u_copies = [
-                remote(usend.at[target], urecv.at[sweep, xy], u_send.at[sweep, index], u_recv.at[sweep, xy], device)
+                remote(usend.at[target, message], urecv.at[sweep, xy, message], u_send.at[sweep, index], u_recv.at[sweep, xy], device)
                 for index, (target, device) in enumerate(plane)
             ]
             send_all(u_copies)
-            urecv[sweep, xy] = usend[xy]
+            urecv[sweep, xy, 0:17] = usend[xy, 0:17]
             if sweep == 0:
                 for group in range(4):
                     for index in range(4):
@@ -349,25 +357,23 @@
                 norms = power
             for source, device in plane:
                 remote(
-                    usend.at[0], urecv.at[sweep, source], u_send.at[sweep, 0], u_recv.at[sweep, source], device
+                    usend.at[0, message], urecv.at[sweep, source, message], u_send.at[sweep, 0], u_recv.at[sweep, source], device
                 ).wait_recv()
-            total = jnp.sum(urecv[sweep], axis=0)
-            squared = jnp.sum(total[16:24], axis=1, keepdims=True)
-            step_size = norms / (squared / tokens_all + DAMPING * power)
-            mine = jnp.sum(jnp.where(query_row == xy // 2, step_size, 0.0), axis=0, keepdims=True)
+            total = jnp.sum(urecv[sweep, :, 0:17], axis=0)
+            squared = jnp.sum(total[16:17], axis=1, keepdims=True)
+            mine = own_query(norms) / (squared / tokens_all + DAMPING * own_query(power))
             own_image = total[0:16] / tokens_all + DAMPING * direction[own_rows, :]
-            rbuf[sweep, own_rows, :] = residual[own_rows, :] - mine * own_image
+            rbuf[sweep, xy, 0:16] = residual[own_rows, :] - mine * own_image
+            rbuf[sweep, xy, 16:17] = jnp.broadcast_to(mine, (1, 128))
             r_copies = [
                 remote(
-                    rbuf.at[sweep, own_rows, :], rbuf.at[sweep, own_rows, :], r_send.at[sweep, index],
+                    rbuf.at[sweep, xy, message], rbuf.at[sweep, xy, message], r_send.at[sweep, index],
                     r_recv.at[sweep, xy], device,
                 )
                 for index, (_, device) in enumerate(plane)
             ]
             send_all(r_copies)
             pending.append(functools.partial(sent_all, r_copies))
-            terms = [step_size * value for value in sums]
-            scores = terms if scores is None else [a + b for a, b in zip(scores, terms)]
             sent_all(u_copies)
             if sweep == 0:
                 @pl.when(owns)
@@ -375,12 +381,14 @@
                     sent_all(b_copies)
 
             for source, device in plane:
-                rows = pl.ds(pl.multiple_of(source * 16, 16), 16)
                 remote(
-                    rbuf.at[sweep, rows, :], rbuf.at[sweep, rows, :], r_send.at[sweep, 0],
+                    rbuf.at[sweep, source, message], rbuf.at[sweep, source, message], r_send.at[sweep, 0],
                     r_recv.at[sweep, source], device,
                 ).wait_recv()
-            left_over = rbuf[sweep]
+            step_size = jnp.concatenate([rbuf[sweep, 2 * query, 16:17] for query in range(8)], axis=0)
+            terms = [step_size * value for value in sums]
+            scores = terms if scores is None else [a + b for a, b in zip(scores, terms)]
+            left_over = rbuf[sweep, :, 0:16].reshape(256, 128)
             residual[...] = left_over
             cube_r = left_over.reshape(8, 32, 128)
             norms_next = query_sum(cube_r * cube_r)
@@ -467,7 +475,7 @@
             pltpu.VMEM((256, 128), F32),
             pltpu.VMEM((16, 24, 128), F32),
             pltpu.VMEM((2, 16, 24, 128), F32),
-            pltpu.VMEM((2, 256, 128), F32),
+            pltpu.VMEM((2, 16, 24, 128), F32),
             pltpu.VMEM((8, 128), F32),
             pltpu.VMEM((16, 8, 128), F32),
             pltpu.VMEM((4, 8, 128), F32),

time: 70 us -> 69.3 us (0.990)
  Pallas kernels: 68.6 us -> 67.8 us
    pallas_call x1, Pallas kernels: 68.6 us -> 67.8 us  [local(): pl.pallas_call(functools.partial(kernel, float(tokens_all)), out_shape=ja...]
where the time goes in v3:
time: 69.3 us; the launch traced here: 69.1 us
  Pallas kernels  67.8 us (98%)
  local copies, waits for them, and re-layouts  1.3 us (2%)
    pallas_call x1, Pallas kernels, local(): pl.pallas_call(functools.partial(kernel, float(tokens_all)), out_shape=ja...  67.8 us

profile of v3, /device:TPU:1, one launch (start us, length us, event | category | flops | bytes accessed | tf_op | source)
XLA Modules:
  0.0 69.1 jit_solution(13002827416049845168)
XLA Ops:
  0.0 67.8 %shard_map.82 = f32[16,128]{1,0:T(8,128)} custom-call(bf16[512,1280]{1,0:T(8,128)(2,1)} %inp.1, bf16[512,6912]{1,0:T(8,128)(2,1)} %outg.1, bf16[128,1280]{1,0:T(8,128)(2,1)} %qinp.1, bf16[128,6912]{1,0:T(8,128)(2,1)} %qoutg.1, bf16[64,1280]{1,0:T(8,128)(2,1)} %bitcast.3, bf16[64,6912]{1,0:T(8,128)(2,1)} %bitcast.2, s32[1,512]{1,0:T(1,128)} %ids_in.1, ...), custom_call_target="tpu_custom_call" | custom-call | tf_op jit(solution)/shard_map/pallas_call | solution.py:448
  67.8 1.3 %copy.10 = f32[16,128]{1,0:T(8,128)} copy(f32[16,128]{1,0:T(8,128)} %shard_map.82) | data formatting | bytes 16384

commit v4 on v3

--- a/solution.py
+++ b/solution.py
@@ -93,10 +93,10 @@
     def project(left, right):
         return jnp.concatenate(
             [
-                lax.dot_general(left, win_v[...], NT, preferred_element_type=F32),
-                lax.dot_general(right, wout_v[...], NT, preferred_element_type=F32),
+                lax.dot_general(win_v[...], left, NT, preferred_element_type=F32),
+                lax.dot_general(wout_v[...], right, NT, preferred_element_type=F32),
             ],
-            axis=1,
+            axis=0,
         )
 
     def project_chunk(step):
@@ -104,8 +104,16 @@
             load.wait()
         part[step] = project(inp_v[step], outg_v[step])
 
+    pieces = [pl.ds(0, 32), pl.ds(32, 32), pl.ds(64, 32), pl.ds(96, 32)]
     rs_copies = [
-        remote(part.at[step], rs.at[zl], rs_send.at[step], rs_recv.at[zl], (dp, owners[step])) for step in range(3)
+        [
+            remote(
+                part.at[step, pieces[piece]], rs.at[zl, pieces[piece]], rs_send.at[step, piece],
+                rs_recv.at[zl, piece], (dp, owners[step]),
+            )
+            for piece in range(4)
+        ]
+        for step in range(3)
     ]
     diag = lax.rem(xpos + ypos, 4)
     query_owner = jnp.where(core == 0, diag, 3 - diag)
@@ -117,10 +125,12 @@
     project_chunk(0)
     project_chunk(1)
     pl.semaphore_wait(barrier, 30)
-    rs_copies[0].start()
-    rs_copies[1].start()
+    for piece in range(4):
+        rs_copies[0][piece].start()
+        rs_copies[1][piece].start()
     project_chunk(2)
-    rs_copies[2].start()
+    for piece in range(4):
+        rs_copies[2][piece].start()
     for index in (1, 3, 4, 5):
         loads[index].wait()
     qpart[...] = project(qinp_v[...], qoutg_v[...])
@@ -137,8 +147,9 @@
         def _():
             q_copy.wait_send()
 
-        for copy in rs_copies:
-            copy.wait_send()
+        for copies in rs_copies:
+            for copy in copies:
+                copy.wait_send()
 
     pending.append(first_done)
 
@@ -147,31 +158,43 @@
         ids_own = ids_own + jnp.where(zl == index, ids[:, index * 128 : (index + 1) * 128].astype(F32), 0.0)
     own = z * 2 + core
     ft[own, 128:136] = jnp.broadcast_to(ids_own, (8, 128))
-    for step in range(1, 4):
-        remote(part.at[0], rs.at[zls[step]], rs_send.at[0], rs_recv.at[zls[step]], (dp, zls[step])).wait_recv()
-    ft[own, 0:128] = ((rs[0] + rs[1]) + (rs[2] + rs[3])).T
-
-    whole, upper, lower = pl.ds(0, 136), pl.ds(0, 64), pl.ds(64, 72)
-
-    def handed(index, origin, rows, target):
-        where = ft.at[lax.rem(z + origin, 8) * 2 + core, rows, :]
-        return remote(where, where, ag_send.at[index], ag_recv.at[index], up_column(target))
+
+    whole = pl.ds(0, 129)
+    pieces[3] = pl.ds(96, 33)
+    halves = (pl.ds(0, 64), pl.ds(64, 65))
+    sent = []
+
+    def start(copy):
+        copy.start()
+        sent.append(copy)
+
+    def handed(kind, piece, origin, target):
+        where = ft.at[lax.rem(z + origin, 8) * 2 + core, pieces[piece], :]
+        return remote(where, where, ag_send.at[kind, piece], ag_recv.at[kind, piece], up_column(target))
 
     def sibling(index, origin, rows, back=False):
         where = ft.at[lax.rem(z + origin, 8) * 2 + (1 - core if back else core), rows, :]
         return remote(where, where, sib_send.at[index], sib_recv.at[index], up_column(0, 1 - core))
 
-    arrivals = ((6, whole), (2, whole), (7, whole), (1, whole), (5, whole), (3, whole), (4, upper), (4, lower))
-    sent = []
-
-    def start(copy):
-        copy.start()
-        sent.append(copy)
-
-    start(handed(0, 0, whole, 2))
-    start(handed(1, 0, whole, 6))
-    start(handed(2, 0, whole, 1))
-    start(handed(3, 0, whole, 7))
+    origins = (6, 2, 7, 1, 5, 3, 4, 4)
+
+    def arrive(kind, piece):
+        handed(kind, piece, origins[kind], 1).wait_recv()
+
+    for piece in range(4):
+        for step in range(1, 4):
+            rows = pl.ds(piece * 32, 32)
+            remote(
+                part.at[0, rows], rs.at[zls[step], rows], rs_send.at[0, piece], rs_recv.at[zls[step], piece],
+                (dp, zls[step]),
+            ).wait_recv()
+        span = slice(piece * 32, piece * 32 + 32)
+        ft[own, span] = (rs[0, span] + rs[1, span]) + (rs[2, span] + rs[3, span])
+        start(handed(0, piece, 0, 2))
+        start(handed(1, piece, 0, 6))
+    for piece in range(4):
+        start(handed(2, piece, 0, 1))
+        start(handed(3, piece, 0, 7))
     start(sibling(8, 0, whole))
 
     lane = lax.broadcasted_iota(jnp.int32, (128, 128), 1)
@@ -186,8 +209,8 @@
         qrs[zl] = qpart[...]
         for step in range(1, 4):
             remote(qpart, qrs.at[zls[step]], q_send, q_recv.at[zls[step]], (dp, zls[step])).wait_recv()
-        feats = (qrs[0] + qrs[1]) + (qrs[2] + qrs[3])
-        turned = feats.T
+        turned = (qrs[0] + qrs[1]) + (qrs[2] + qrs[3])
+        feats = turned.T
         right = jnp.concatenate(
             [jnp.where(lane < 64, pltpu.roll(feats, 64, 1), 0.0), jnp.where(lane >= 64, feats, 0.0)], axis=0
         )
@@ -201,25 +224,20 @@
         for copy in b_copies:
             copy.start()
 
-    def arrive(index):
-        origin, rows = arrivals[index]
-        handed(index, origin, rows, 1).wait_recv()
-
-    def pass_on(index):
-        origin, rows = arrivals[index]
-        start(sibling(index, origin, rows))
-
-    arrive(0)
-    start(handed(4, 6, whole, 1))
-    start(handed(6, 6, upper, 2))
-    pass_on(0)
-    arrive(1)
-    start(handed(5, 2, whole, 7))
-    start(handed(7, 2, lower, 6))
-    pass_on(1)
-    for index in (2, 3):
-        arrive(index)
-        pass_on(index)
+    for piece in range(4):
+        arrive(0, piece)
+        start(handed(4, piece, 6, 1))
+        if piece < 2:
+            start(handed(6, piece, 6, 2))
+        arrive(1, piece)
+        start(handed(5, piece, 2, 7))
+        if piece >= 2:
+            start(handed(7, piece, 2, 6))
+    for kind in range(4):
+        if kind >= 2:
+            for piece in range(4):
+                arrive(kind, piece)
+        start(sibling(kind, origins[kind], whole))
 
     def prepare(tile):
         both = jnp.concatenate([ft[2 * tile], ft[2 * tile + 1]], axis=1)
@@ -235,13 +253,16 @@
             axis=1,
         )
 
-    def sibling_tile(index, origin, rows=whole):
-        sibling(index, origin, rows, True).wait_recv()
-
     near = [(8, 0), (0, 6), (1, 2), (2, 7), (3, 1)]
     for index, origin in near:
-        sibling_tile(index, origin)
+        sibling(index, origin, whole, True).wait_recv()
         prepare(lax.rem(z + origin, 8))
+    far = [(4, 5, 0), (5, 3, 0), (6, 4, 0), (9, 5, 1), (10, 3, 1), (7, 4, 1)]
+    for index, origin, side in far:
+        kind = {5: 4, 3: 5, 4: 6 + side}[origin]
+        for piece in (2 * side, 2 * side + 1):
+            arrive(kind, piece)
+        start(sibling(index, origin, halves[side]))
 
     for source in range(4):
         @pl.when(jnp.logical_not(jnp.logical_and(owns, ypos == source)))
@@ -319,16 +340,10 @@
         if sweep == 0:
             for place, (_, origin) in enumerate(near):
                 squares = product(lax.rem(z + origin, 8), squares, place == 0, True)
-            for index in range(4, 8):
-                arrive(index)
-                pass_on(index)
-            sibling_tile(4, 5)
-            prepare(lax.rem(z + 5, 8))
-            sibling_tile(5, 3)
-            prepare(lax.rem(z + 3, 8))
-            sibling_tile(6, 4, upper)
-            sibling_tile(7, 4, lower)
-            prepare(lax.rem(z + 4, 8))
+            for index, origin, side in far:
+                sibling(index, origin, halves[side], True).wait_recv()
+            for origin in (5, 3, 4):
+                prepare(lax.rem(z + origin, 8))
             for origin in (5, 3, 4):
                 squares = product(lax.rem(z + origin, 8), squares, False, True)
         else:
@@ -482,14 +497,14 @@
             pltpu.VMEM((16, 8, 128), F32),
             pltpu.VMEM((128, 128), F32),
             dma((14,)),
-            dma((4,)),
-            dma((4,)),
+            dma((3, 4)),
+            dma((4, 4)),
             dma,
             dma((4,)),
-            dma((8,)),
-            dma((8,)),
-            dma((9,)),
-            dma((9,)),
+            dma((8, 4)),
+            dma((8, 4)),
+            dma((11,)),
+            dma((11,)),
             dma((16,)),
             dma((4,)),
             dma((2, 16)),

time: 69.3 us -> 69.2 us (level)
  no operation moved by 1% of the time
where the time goes in v4:
time: 69.2 us; the launch traced here: 69 us
  Pallas kernels  67.7 us (98%)
  local copies, waits for them, and re-layouts  1.3 us (2%)
    pallas_call x1, Pallas kernels, local(): pl.pallas_call(functools.partial(kernel, float(tokens_all)), out_shape=ja...  67.7 us

profile of v4, /device:TPU:1, one launch (start us, length us, event | category | flops | bytes accessed | tf_op | source)
XLA Modules:
  0.0 69.0 jit_solution(8843347612287264811)
XLA Ops:
  0.0 67.7 %shard_map.82 = f32[16,128]{1,0:T(8,128)} custom-call(bf16[512,1280]{1,0:T(8,128)(2,1)} %inp.1, bf16[512,6912]{1,0:T(8,128)(2,1)} %outg.1, bf16[128,1280]{1,0:T(8,128)(2,1)} %qinp.1, bf16[128,6912]{1,0:T(8,128)(2,1)} %qoutg.1, bf16[64,1280]{1,0:T(8,128)(2,1)} %bitcast.3, bf16[64,6912]{1,0:T(8,128)(2,1)} %bitcast.2, s32[1,512]{1,0:T(1,128)} %ids_in.1, ...), custom_call_target="tpu_custom_call" | custom-call | tf_op jit(solution)/shard_map/pallas_call | solution.py:463
  67.7 1.3 %copy.10 = f32[16,128]{1,0:T(8,128)} copy(f32[16,128]{1,0:T(8,128)} %shard_map.82) | data formatting | bytes 16384

commit v5 on v4

--- a/solution.py
+++ b/solution.py
@@ -30,7 +30,7 @@
     out,
     ids, qids, win_v, wout_v, inp_v, outg_v, qinp_v, qoutg_v,
     part, qpart, rs, qrs, ft, rhs1, rhs2, feat_a, lhs, wbuf, acc, onehot,
-    direction, residual, usend, urecv, rbuf, ssend, srecv, fsend, frecv, order,
+    direction, residual, usend, urecv, rbuf, ssend, srecv, fsend, frecv, order, lined,
     load_sem, rs_send, rs_recv, q_send, q_recv, ag_send, ag_recv, sib_send, sib_recv,
     b_send, b_recv, u_send, u_recv, r_send, r_recv, s_send, s_recv, f_send, f_recv,
 ):
@@ -82,13 +82,13 @@
                 pltpu.make_async_copy(outg.at[rows, :], outg_v.at[step], load_sem.at[8 + step]),
             )
         )
-    loads[0].start()
-    loads[2].start()
-    for pair in chunk_loads:
-        for load in pair:
+    def begin(some):
+        for load in some:
             load.start()
-    for index in (1, 3, 4, 5):
-        loads[index].start()
+
+    begin((loads[0], loads[2]))
+    begin(chunk_loads[0])
+    begin((loads[1], loads[3], loads[4], loads[5]))
 
     def project(left, right):
         return jnp.concatenate(
@@ -123,22 +123,24 @@
     loads[0].wait()
     loads[2].wait()
     project_chunk(0)
-    project_chunk(1)
-    pl.semaphore_wait(barrier, 30)
-    for piece in range(4):
-        rs_copies[0][piece].start()
-        rs_copies[1][piece].start()
-    project_chunk(2)
-    for piece in range(4):
-        rs_copies[2][piece].start()
+    begin(chunk_loads[1])
+    begin(chunk_loads[2])
     for index in (1, 3, 4, 5):
         loads[index].wait()
     qpart[...] = project(qinp_v[...], qoutg_v[...])
+    begin(chunk_loads[3])
+    pl.semaphore_wait(barrier, 30)
+    for copy in rs_copies[0]:
+        copy.start()
 
     @pl.when(jnp.logical_not(owns))
     def _():
         q_copy.start()
 
+    for step in (1, 2):
+        project_chunk(step)
+        for copy in rs_copies[step]:
+            copy.start()
     project_chunk(3)
     rs[zl] = part[3]
 
@@ -152,50 +154,6 @@
                 copy.wait_send()
 
     pending.append(first_done)
-
-    ids_own = jnp.zeros((1, 128), F32)
-    for index in range(4):
-        ids_own = ids_own + jnp.where(zl == index, ids[:, index * 128 : (index + 1) * 128].astype(F32), 0.0)
-    own = z * 2 + core
-    ft[own, 128:136] = jnp.broadcast_to(ids_own, (8, 128))
-
-    whole = pl.ds(0, 129)
-    pieces[3] = pl.ds(96, 33)
-    halves = (pl.ds(0, 64), pl.ds(64, 65))
-    sent = []
-
-    def start(copy):
-        copy.start()
-        sent.append(copy)
-
-    def handed(kind, piece, origin, target):
-        where = ft.at[lax.rem(z + origin, 8) * 2 + core, pieces[piece], :]
-        return remote(where, where, ag_send.at[kind, piece], ag_recv.at[kind, piece], up_column(target))
-
-    def sibling(index, origin, rows, back=False):
-        where = ft.at[lax.rem(z + origin, 8) * 2 + (1 - core if back else core), rows, :]
-        return remote(where, where, sib_send.at[index], sib_recv.at[index], up_column(0, 1 - core))
-
-    origins = (6, 2, 7, 1, 5, 3, 4, 4)
-
-    def arrive(kind, piece):
-        handed(kind, piece, origins[kind], 1).wait_recv()
-
-    for piece in range(4):
-        for step in range(1, 4):
-            rows = pl.ds(piece * 32, 32)
-            remote(
-                part.at[0, rows], rs.at[zls[step], rows], rs_send.at[0, piece], rs_recv.at[zls[step], piece],
-                (dp, zls[step]),
-            ).wait_recv()
-        span = slice(piece * 32, piece * 32 + 32)
-        ft[own, span] = (rs[0, span] + rs[1, span]) + (rs[2, span] + rs[3, span])
-        start(handed(0, piece, 0, 2))
-        start(handed(1, piece, 0, 6))
-    for piece in range(4):
-        start(handed(2, piece, 0, 1))
-        start(handed(3, piece, 0, 7))
-    start(sibling(8, 0, whole))
 
     lane = lax.broadcasted_iota(jnp.int32, (128, 128), 1)
     pair_rows = pl.ds(pl.multiple_of(ypos * 64, 64), 64)
@@ -223,6 +181,50 @@
         )
         for copy in b_copies:
             copy.start()
+
+    ids_own = jnp.zeros((1, 128), F32)
+    for index in range(4):
+        ids_own = ids_own + jnp.where(zl == index, ids[:, index * 128 : (index + 1) * 128].astype(F32), 0.0)
+    own = z * 2 + core
+    ft[own, 128:136] = jnp.broadcast_to(ids_own, (8, 128))
+
+    whole = pl.ds(0, 129)
+    pieces[3] = pl.ds(96, 33)
+    halves = (pl.ds(0, 64), pl.ds(64, 65))
+    sent = []
+
+    def start(copy):
+        copy.start()
+        sent.append(copy)
+
+    def handed(kind, piece, origin, target):
+        where = ft.at[lax.rem(z + origin, 8) * 2 + core, pieces[piece], :]
+        return remote(where, where, ag_send.at[kind, piece], ag_recv.at[kind, piece], up_column(target))
+
+    def sibling(index, origin, rows, back=False):
+        where = ft.at[lax.rem(z + origin, 8) * 2 + (1 - core if back else core), rows, :]
+        return remote(where, where, sib_send.at[index], sib_recv.at[index], up_column(0, 1 - core))
+
+    origins = (6, 2, 7, 1, 5, 3, 4, 4)
+
+    def arrive(kind, piece):
+        handed(kind, piece, origins[kind], 1).wait_recv()
+
+    for piece in range(4):
+        for step in range(1, 4):
+            rows = pl.ds(piece * 32, 32)
+            remote(
+                part.at[0, rows], rs.at[zls[step], rows], rs_send.at[0, piece], rs_recv.at[zls[step], piece],
+                (dp, zls[step]),
+            ).wait_recv()
+        span = slice(piece * 32, piece * 32 + 32)
+        ft[own, span] = (rs[0, span] + rs[1, span]) + (rs[2, span] + rs[3, span])
+        start(handed(0, piece, 0, 2))
+        start(handed(1, piece, 0, 6))
+    for piece in range(4):
+        start(handed(2, piece, 0, 1))
+        start(handed(3, piece, 0, 7))
+    start(sibling(8, 0, whole))
 
     for piece in range(4):
         arrive(0, piece)
@@ -427,31 +429,38 @@
     step_size = norms / (squared / tokens_all + DAMPING * power)
 
     for group in range(4):
-        fsend[group] = (scores[group] + step_size * sums[group]) * (1.0 / 4096)
+        made = jnp.where(lane[0:8] < 16, (scores[group] + step_size * sums[group]) * (1.0 / 4096), 0.0)
+        turned = [made[0:1]] + [pltpu.roll(made[query : query + 1], 16 * query, 1) for query in range(1, 8)]
+        row = (turned[0] + turned[1]) + (turned[2] + turned[3]) + ((turned[4] + turned[5]) + (turned[6] + turned[7]))
+        fsend[group, 0:1] = row
 
     def f_slot(where, height):
         return jnp.where(lax.rem(where, 2) == 0, height, 3 - height) * 4 + where
 
     own_slot = f_slot(low, zl)
+    one_row = pl.ds(0, 1)
     f_copies = [
-        remote(fsend.at[where], frecv.at[own_slot], f_send.at[index], f_recv.at[own_slot], device)
+        remote(fsend.at[where, one_row], frecv.at[own_slot, one_row], f_send.at[index], f_recv.at[own_slot], device)
         for index, (where, _, device) in enumerate(column)
     ]
     send_all(f_copies)
     pending.append(functools.partial(sent_all, f_copies))
-    frecv[own_slot] = fsend[low]
+    frecv[own_slot, 0:1] = fsend[low, 0:1]
     for copy in sent:
         copy.wait_send()
     for done in pending:
         done()
     for where, height, device in column:
         slot = f_slot(where, height)
-        remote(fsend.at[0], frecv.at[slot], f_send.at[0], f_recv.at[slot], device).wait_recv()
+        remote(fsend.at[0, one_row], frecv.at[slot, one_row], f_send.at[0], f_recv.at[slot], device).wait_recv()
     for where in range(16):
-        diagonal, rest = where // 4, where % 4
-        for row in range(4):
-            begin = row * 32 + ((diagonal - row) % 4) * 8 + rest * 2
-            order[begin : begin + 2] = frecv[where, 2 * row : 2 * row + 2]
+        lined[where : where + 1] = frecv[where, 0:1]
+    for query in range(8):
+        row, which = query // 2, query % 2
+        places = lined[...] if query == 0 else pltpu.roll(lined[...], 128 - 16 * query, 1)
+        for diagonal in range(4):
+            begin_row = row * 32 + ((diagonal - row) % 4) * 8 + which
+            order[pl.ds(begin_row, 4, stride=2)] = places[4 * diagonal : 4 * diagonal + 4]
     out[...] = order[...].T[0:16]
 
 
@@ -496,6 +505,7 @@
             pltpu.VMEM((4, 8, 128), F32),
             pltpu.VMEM((16, 8, 128), F32),
             pltpu.VMEM((128, 128), F32),
+            pltpu.VMEM((16, 128), F32),
             dma((14,)),
             dma((3, 4)),
             dma((4, 4)),

time: 69.2 us -> 69.3 us (level)
  no operation moved by 1% of the time
where the time goes in v5:
time: 69.3 us; the launch traced here: 69.1 us
  Pallas kernels  67.8 us (98%)
  local copies, waits for them, and re-layouts  1.3 us (2%)
    pallas_call x1, Pallas kernels, local(): pl.pallas_call(functools.partial(kernel, float(tokens_all)), out_shape=ja...  67.8 us

profile of v5, /device:TPU:1, one launch (start us, length us, event | category | flops | bytes accessed | tf_op | source)
XLA Modules:
  0.0 69.1 jit_solution(14602523541125777657)
XLA Ops:
  0.0 67.8 %shard_map.82 = f32[16,128]{1,0:T(8,128)} custom-call(bf16[512,1280]{1,0:T(8,128)(2,1)} %inp.1, bf16[512,6912]{1,0:T(8,128)(2,1)} %outg.1, bf16[128,1280]{1,0:T(8,128)(2,1)} %qinp.1, bf16[128,6912]{1,0:T(8,128)(2,1)} %qoutg.1, bf16[64,1280]{1,0:T(8,128)(2,1)} %bitcast.3, bf16[64,6912]{1,0:T(8,128)(2,1)} %bitcast.2, s32[1,512]{1,0:T(1,128)} %ids_in.1, ...), custom_call_target="tpu_custom_call" | custom-call | tf_op jit(solution)/shard_map/pallas_call | solution.py:472
  67.8 1.3 %copy.10 = f32[16,128]{1,0:T(8,128)} copy(f32[16,128]{1,0:T(8,128)} %shard_map.82) | data formatting | bytes 16384

commit v6 on v4

--- a/solution.py
+++ b/solution.py
@@ -30,7 +30,7 @@
     out,
     ids, qids, win_v, wout_v, inp_v, outg_v, qinp_v, qoutg_v,
     part, qpart, rs, qrs, ft, rhs1, rhs2, feat_a, lhs, wbuf, acc, onehot,
-    direction, residual, usend, urecv, rbuf, ssend, srecv, fsend, frecv, order,
+    direction, residual, usend, urecv, rbuf, ssend, srecv, fsend, frecv, order, lined,
     load_sem, rs_send, rs_recv, q_send, q_recv, ag_send, ag_recv, sib_send, sib_recv,
     b_send, b_recv, u_send, u_recv, r_send, r_recv, s_send, s_recv, f_send, f_recv,
 ):
@@ -82,13 +82,13 @@
                 pltpu.make_async_copy(outg.at[rows, :], outg_v.at[step], load_sem.at[8 + step]),
             )
         )
-    loads[0].start()
-    loads[2].start()
-    for pair in chunk_loads:
-        for load in pair:
+    def begin(some):
+        for load in some:
             load.start()
-    for index in (1, 3, 4, 5):
-        loads[index].start()
+
+    begin((loads[0], loads[2]))
+    begin(chunk_loads[0])
+    begin((loads[1], loads[3], loads[4], loads[5]))
 
     def project(left, right):
         return jnp.concatenate(
@@ -123,22 +123,26 @@
     loads[0].wait()
     loads[2].wait()
     project_chunk(0)
-    project_chunk(1)
-    pl.semaphore_wait(barrier, 30)
-    for piece in range(4):
-        rs_copies[0][piece].start()
-        rs_copies[1][piece].start()
-    project_chunk(2)
-    for piece in range(4):
-        rs_copies[2][piece].start()
+    begin(chunk_loads[1])
+    begin(chunk_loads[2])
     for index in (1, 3, 4, 5):
         loads[index].wait()
     qpart[...] = project(qinp_v[...], qoutg_v[...])
+    begin(chunk_loads[3])
+    project_chunk(1)
+    pl.semaphore_wait(barrier, 30)
+    for copy in rs_copies[0]:
+        copy.start()
 
     @pl.when(jnp.logical_not(owns))
     def _():
         q_copy.start()
 
+    for copy in rs_copies[1]:
+        copy.start()
+    project_chunk(2)
+    for copy in rs_copies[2]:
+        copy.start()
     project_chunk(3)
     rs[zl] = part[3]
 
@@ -427,31 +431,38 @@
     step_size = norms / (squared / tokens_all + DAMPING * power)
 
     for group in range(4):
-        fsend[group] = (scores[group] + step_size * sums[group]) * (1.0 / 4096)
+        made = jnp.where(lane_row[0:8] < 16, (scores[group] + step_size * sums[group]) * (1.0 / 4096), 0.0)
+        turned = [made[0:1]] + [pltpu.roll(made[query : query + 1], 16 * query, 1) for query in range(1, 8)]
+        row = (turned[0] + turned[1]) + (turned[2] + turned[3]) + ((turned[4] + turned[5]) + (turned[6] + turned[7]))
+        fsend[group, 0:1] = row
 
     def f_slot(where, height):
         return jnp.where(lax.rem(where, 2) == 0, height, 3 - height) * 4 + where
 
     own_slot = f_slot(low, zl)
+    one_row = pl.ds(0, 1)
     f_copies = [
-        remote(fsend.at[where], frecv.at[own_slot], f_send.at[index], f_recv.at[own_slot], device)
+        remote(fsend.at[where, one_row], frecv.at[own_slot, one_row], f_send.at[index], f_recv.at[own_slot], device)
         for index, (where, _, device) in enumerate(column)
     ]
     send_all(f_copies)
     pending.append(functools.partial(sent_all, f_copies))
-    frecv[own_slot] = fsend[low]
+    frecv[own_slot, 0:1] = fsend[low, 0:1]
     for copy in sent:
         copy.wait_send()
     for done in pending:
         done()
     for where, height, device in column:
         slot = f_slot(where, height)
-        remote(fsend.at[0], frecv.at[slot], f_send.at[0], f_recv.at[slot], device).wait_recv()
+        remote(fsend.at[0, one_row], frecv.at[slot, one_row], f_send.at[0], f_recv.at[slot], device).wait_recv()
     for where in range(16):
-        diagonal, rest = where // 4, where % 4
-        for row in range(4):
-            begin = row * 32 + ((diagonal - row) % 4) * 8 + rest * 2
-            order[begin : begin + 2] = frecv[where, 2 * row : 2 * row + 2]
+        lined[where : where + 1] = frecv[where, 0:1]
+    for query in range(8):
+        row, which = query // 2, query % 2
+        places = lined[...] if query == 0 else pltpu.roll(lined[...], 128 - 16 * query, 1)
+        for diagonal in range(4):
+            begin_row = row * 32 + ((diagonal - row) % 4) * 8 + which
+            order[pl.ds(begin_row, 4, stride=2)] = places[4 * diagonal : 4 * diagonal + 4]
     out[...] = order[...].T[0:16]
 
 
@@ -496,6 +507,7 @@
             pltpu.VMEM((4, 8, 128), F32),
             pltpu.VMEM((16, 8, 128), F32),
             pltpu.VMEM((128, 128), F32),
+            pltpu.VMEM((16, 128), F32),
             dma((14,)),
             dma((3, 4)),
             dma((4, 4)),

time: 69.2 us -> 70.3 us (1.016)
  Pallas kernels: 67.7 us -> 68.8 us
    pallas_call x1, Pallas kernels: 67.7 us -> 68.8 us  [local(): pl.pallas_call(functools.partial(kernel, float(tokens_all)), out_shape=ja...]
where the time goes in v6:
time: 70.3 us; the launch traced here: 70.1 us
  Pallas kernels  68.8 us (98%)
  local copies, waits for them, and re-layouts  1.3 us (2%)
    pallas_call x1, Pallas kernels, local(): pl.pallas_call(functools.partial(kernel, float(tokens_all)), out_shape=ja...  68.8 us

profile of v6, /device:TPU:1, one launch (start us, length us, event | category | flops | bytes accessed | tf_op | source)
XLA Modules:
  0.0 70.1 jit_solution(13965516822029870772)
XLA Ops:
  0.0 68.8 %shard_map.82 = f32[16,128]{1,0:T(8,128)} custom-call(bf16[512,1280]{1,0:T(8,128)(2,1)} %inp.1, bf16[512,6912]{1,0:T(8,128)(2,1)} %outg.1, bf16[128,1280]{1,0:T(8,128)(2,1)} %qinp.1, bf16[128,6912]{1,0:T(8,128)(2,1)} %qoutg.1, bf16[64,1280]{1,0:T(8,128)(2,1)} %bitcast.3, bf16[64,6912]{1,0:T(8,128)(2,1)} %bitcast.2, s32[1,512]{1,0:T(1,128)} %ids_in.1, ...), custom_call_target="tpu_custom_call" | custom-call | tf_op jit(solution)/shard_map/pallas_call | solution.py:474
  68.8 1.3 %copy.10 = f32[16,128]{1,0:T(8,128)} copy(f32[16,128]{1,0:T(8,128)} %shard_map.82) | data formatting | bytes 16384

commit v7 on v4

--- a/solution.py
+++ b/solution.py
@@ -30,7 +30,7 @@
     out,
     ids, qids, win_v, wout_v, inp_v, outg_v, qinp_v, qoutg_v,
     part, qpart, rs, qrs, ft, rhs1, rhs2, feat_a, lhs, wbuf, acc, onehot,
-    direction, residual, usend, urecv, rbuf, ssend, srecv, fsend, frecv, order,
+    direction, residual, usend, urecv, rbuf, ssend, srecv, fsend, frecv, order, lined,
     load_sem, rs_send, rs_recv, q_send, q_recv, ag_send, ag_recv, sib_send, sib_recv,
     b_send, b_recv, u_send, u_recv, r_send, r_recv, s_send, s_recv, f_send, f_recv,
 ):
@@ -331,7 +331,7 @@
 
     residual[...] = direction[...]
     norms = None
-    scores = None
+    every_sum = []
     for sweep in range(ITERS):
         last = sweep == ITERS - 1
         vector = direction[...]
@@ -400,9 +400,7 @@
                     rbuf.at[sweep, source, message], rbuf.at[sweep, source, message], r_send.at[sweep, 0],
                     r_recv.at[sweep, source], device,
                 ).wait_recv()
-            step_size = jnp.concatenate([rbuf[sweep, 2 * query, 16:17] for query in range(8)], axis=0)
-            terms = [step_size * value for value in sums]
-            scores = terms if scores is None else [a + b for a, b in zip(scores, terms)]
+            every_sum.append(sums)
             left_over = rbuf[sweep, :, 0:16].reshape(256, 128)
             residual[...] = left_over
             cube_r = left_over.reshape(8, 32, 128)
@@ -421,37 +419,49 @@
     srecv[xy] = squares
     power = query_sum(cube * cube)
     sums = document_sums()
+    scores = None
+    for sweep in range(ITERS - 1):
+        step_size = jnp.concatenate([rbuf[sweep, 2 * query, 16:17] for query in range(8)], axis=0)
+        terms = [step_size * value for value in every_sum[sweep]]
+        scores = terms if scores is None else [a + b for a, b in zip(scores, terms)]
     for source, device in plane:
         remote(ssend, srecv.at[source], s_send.at[0], s_recv.at[source], device).wait_recv()
     squared = jnp.sum(jnp.sum(srecv[...], axis=0), axis=1, keepdims=True)
     step_size = norms / (squared / tokens_all + DAMPING * power)
 
     for group in range(4):
-        fsend[group] = (scores[group] + step_size * sums[group]) * (1.0 / 4096)
+        made = jnp.where(lane_row[0:8] < 16, (scores[group] + step_size * sums[group]) * (1.0 / 4096), 0.0)
+        turned = [made[0:1]] + [pltpu.roll(made[query : query + 1], 16 * query, 1) for query in range(1, 8)]
+        row = (turned[0] + turned[1]) + (turned[2] + turned[3]) + ((turned[4] + turned[5]) + (turned[6] + turned[7]))
+        fsend[group, 0:1] = row
 
     def f_slot(where, height):
         return jnp.where(lax.rem(where, 2) == 0, height, 3 - height) * 4 + where
 
     own_slot = f_slot(low, zl)
+    one_row = pl.ds(0, 1)
     f_copies = [
-        remote(fsend.at[where], frecv.at[own_slot], f_send.at[index], f_recv.at[own_slot], device)
+        remote(fsend.at[where, one_row], frecv.at[own_slot, one_row], f_send.at[index], f_recv.at[own_slot], device)
         for index, (where, _, device) in enumerate(column)
     ]
     send_all(f_copies)
     pending.append(functools.partial(sent_all, f_copies))
-    frecv[own_slot] = fsend[low]
+    frecv[own_slot, 0:1] = fsend[low, 0:1]
     for copy in sent:
         copy.wait_send()
     for done in pending:
         done()
     for where, height, device in column:
         slot = f_slot(where, height)
-        remote(fsend.at[0], frecv.at[slot], f_send.at[0], f_recv.at[slot], device).wait_recv()
+        remote(fsend.at[0, one_row], frecv.at[slot, one_row], f_send.at[0], f_recv.at[slot], device).wait_recv()
     for where in range(16):
-        diagonal, rest = where // 4, where % 4
-        for row in range(4):
-            begin = row * 32 + ((diagonal - row) % 4) * 8 + rest * 2
-            order[begin : begin + 2] = frecv[where, 2 * row : 2 * row + 2]
+        lined[where : where + 1] = frecv[where, 0:1]
+    for query in range(8):
+        row, which = query // 2, query % 2
+        places = lined[...] if query == 0 else pltpu.roll(lined[...], 128 - 16 * query, 1)
+        for diagonal in range(4):
+            begin_row = row * 32 + ((diagonal - row) % 4) * 8 + which
+            order[pl.ds(begin_row, 4, stride=2)] = places[4 * diagonal : 4 * diagonal + 4]
     out[...] = order[...].T[0:16]
 
 
@@ -496,6 +506,7 @@
             pltpu.VMEM((4, 8, 128), F32),
             pltpu.VMEM((16, 8, 128), F32),
             pltpu.VMEM((128, 128), F32),
+            pltpu.VMEM((16, 128), F32),
             dma((14,)),
             dma((3, 4)),
             dma((4, 4)),

time: 69.2 us -> 69 us (level)
  no operation moved by 1% of the time
where the time goes in v7:
time: 69 us; the launch traced here: 68.8 us
  Pallas kernels  67.5 us (98%)
  local copies, waits for them, and re-layouts  1.3 us (2%)
    pallas_call x1, Pallas kernels, local(): pl.pallas_call(functools.partial(kernel, float(tokens_all)), out_shape=ja...  67.5 us

profile of v7, /device:TPU:1, one launch (start us, length us, event | category | flops | bytes accessed | tf_op | source)
XLA Modules:
  0.0 68.8 jit_solution(9085731797797900374)
XLA Ops:
  0.0 67.5 %shard_map.82 = f32[16,128]{1,0:T(8,128)} custom-call(bf16[512,1280]{1,0:T(8,128)(2,1)} %inp.1, bf16[512,6912]{1,0:T(8,128)(2,1)} %outg.1, bf16[128,1280]{1,0:T(8,128)(2,1)} %qinp.1, bf16[128,6912]{1,0:T(8,128)(2,1)} %qoutg.1, bf16[64,1280]{1,0:T(8,128)(2,1)} %bitcast.3, bf16[64,6912]{1,0:T(8,128)(2,1)} %bitcast.2, s32[1,512]{1,0:T(1,128)} %ids_in.1, ...), custom_call_target="tpu_custom_call" | custom-call | tf_op jit(solution)/shard_map/pallas_call | solution.py:473
  67.5 1.3 %copy.10 = f32[16,128]{1,0:T(8,128)} copy(f32[16,128]{1,0:T(8,128)} %shard_map.82) | data formatting | bytes 16384

commit v8 on v7

--- a/solution.py
+++ b/solution.py
@@ -192,9 +192,6 @@
         ft[own, span] = (rs[0, span] + rs[1, span]) + (rs[2, span] + rs[3, span])
         start(handed(0, piece, 0, 2))
         start(handed(1, piece, 0, 6))
-    for piece in range(4):
-        start(handed(2, piece, 0, 1))
-        start(handed(3, piece, 0, 7))
     start(sibling(8, 0, whole))
 
     lane = lax.broadcasted_iota(jnp.int32, (128, 128), 1)
@@ -233,6 +230,10 @@
         start(handed(5, piece, 2, 7))
         if piece >= 2:
             start(handed(7, piece, 2, 6))
+        if piece == 0:
+            for near_piece in range(4):
+                start(handed(2, near_piece, 0, 1))
+                start(handed(3, near_piece, 0, 7))
     for kind in range(4):
         if kind >= 2:
             for piece in range(4):

time: 69 us -> 69.3 us (level)
  no operation moved by 1% of the time
where the time goes in v8:
time: 69.3 us; the launch traced here: 69.2 us
  Pallas kernels  67.9 us (98%)
  local copies, waits for them, and re-layouts  1.3 us (2%)
    pallas_call x1, Pallas kernels, local(): pl.pallas_call(functools.partial(kernel, float(tokens_all)), out_shape=ja...  67.9 us

profile of v8, /device:TPU:1, one launch (start us, length us, event | category | flops | bytes accessed | tf_op | source)
XLA Modules:
  0.0 69.2 jit_solution(16641135416283008585)
XLA Ops:
  0.0 67.9 %shard_map.82 = f32[16,128]{1,0:T(8,128)} custom-call(bf16[512,1280]{1,0:T(8,128)(2,1)} %inp.1, bf16[512,6912]{1,0:T(8,128)(2,1)} %outg.1, bf16[128,1280]{1,0:T(8,128)(2,1)} %qinp.1, bf16[128,6912]{1,0:T(8,128)(2,1)} %qoutg.1, bf16[64,1280]{1,0:T(8,128)(2,1)} %bitcast.3, bf16[64,6912]{1,0:T(8,128)(2,1)} %bitcast.2, s32[1,512]{1,0:T(1,128)} %ids_in.1, ...), custom_call_target="tpu_custom_call" | custom-call | tf_op jit(solution)/shard_map/pallas_call | solution.py:474
  67.9 1.3 %copy.10 = f32[16,128]{1,0:T(8,128)} copy(f32[16,128]{1,0:T(8,128)} %shard_map.82) | data formatting | bytes 16384
